TPU v7x, 128 devices: a whole 4x4x4 slice. The times are simulated.
128 devices in a mesh: wide: 8 (over x, core), narrow: 16 (over z, y).
Axes of the slice: x: 4, y: 4, z: 4, core: 2. Of those that a mesh axis runs over, the one named last changes fastest.
Arguments:
- view_a: bfloat16 [1024, 8192], P(('wide', 'narrow')), may hold values from -20000 to 20000, as said below
- view_b: bfloat16 [1024, 8192], P(('wide', 'narrow')), may hold values from -20000 to 20000
Outputs:
- corr: bfloat16 [8192, 8192], P('wide', 'narrow')
- loss_value: float32 [], replicated
- grad_a: bfloat16 [1024, 8192], P(('wide', 'narrow'))
- grad_b: bfloat16 [1024, 8192], P(('wide', 'narrow'))
Inputs may be any that keep to these rules, and one draw needn't show every extreme that they name: view_b shows the same images as view_a under another augmentation.
All inputs are finite; a program needn't handle non-finite values.
Results may differ from a plain program's by a relative error of at most 0.019.
Values may be sent and summed in bfloat16 or wider, within the bound.
A program may use at most 64 MiB of HBM per device.

v0:
```python
import jax
import jax.numpy as jnp
from jax import lax
from jax.sharding import PartitionSpec as P

off_weight = 0.0051
epsilon = 1e-05


def from_behind(shard, axis, by):
    peers = lax.axis_size(axis)
    return lax.ppermute(shard, axis, [(i, (i + by) % peers) for i in range(peers)])


def block_weights(cross_corr, diag_mask):
    scaled = 2.0 * off_weight * cross_corr
    return (
        scaled + diag_mask * (-2.0 * (1.0 - cross_corr) - 2.0 * off_weight * cross_corr)
    ).astype(jnp.bfloat16)


def block_loss(cross_corr, diag_mask):
    return jnp.sum(
        jnp.where(
            diag_mask > 0.5,
            (1.0 - cross_corr) * (1.0 - cross_corr),
            off_weight * cross_corr * cross_corr,
        )
    )


def pair_slabs(first_view, second_view, wide_size):
    row_count = first_view.shape[0]
    return jnp.concatenate(
        [
            first_view.reshape(row_count, wide_size, -1),
            second_view.reshape(row_count, wide_size, -1),
        ],
        axis=2,
    )


def on_device(view_a, view_b):
    row_count, features = view_a.shape
    wide_size = lax.axis_size("wide")
    narrow_size = lax.axis_size("narrow")
    slab = features // wide_size
    sub_cols = slab // narrow_size
    samples = row_count * wide_size * narrow_size
    quarter = row_count * wide_size
    wide_index = lax.axis_index("wide")
    narrow_index = lax.axis_index("narrow")
    floats_a = view_a.astype(jnp.float32)
    floats_b = view_b.astype(jnp.float32)
    totals = lax.psum(
        jnp.stack(
            [
                jnp.sum(floats_a, axis=0),
                jnp.sum(floats_b, axis=0),
                jnp.sum(floats_a * floats_a, axis=0),
                jnp.sum(floats_b * floats_b, axis=0),
            ]
        ),
        ("wide", "narrow"),
    )
    average = totals[0:2] / samples
    variance = totals[2:4] / samples - average * average
    inv_std = lax.rsqrt(variance + epsilon)
    std_a = ((floats_a - average[0]) * inv_std[0]).astype(jnp.bfloat16)
    std_b = ((floats_b - average[1]) * inv_std[1]).astype(jnp.bfloat16)
    outgoing = pair_slabs(std_a, std_b, wide_size)
    arrived = lax.all_to_all(outgoing, "wide", split_axis=1, concat_axis=0, tiled=True).reshape(
        quarter, 2 * slab
    )
    inv_own = lax.dynamic_slice(inv_std, (0, wide_index * slab), (2, slab)).reshape(2 * slab)
    contract_rows = (((0,), (0,)), ((), ()))
    contract_cols = (((1,), (1,)), ((), ()))
    full_slab = lax.all_gather(arrived, "narrow", axis=0, tiled=True)
    slab_pos = jnp.arange(slab)
    sub_pos = narrow_index * sub_cols + jnp.arange(sub_cols)
    full_a = full_slab[:, :slab]
    full_b = full_slab[:, slab:]
    first_visit = jnp.concatenate(
        [
            lax.dynamic_slice_in_dim(full_slab, narrow_index * sub_cols, sub_cols, 1),
            lax.dynamic_slice_in_dim(full_slab, slab + narrow_index * sub_cols, sub_cols, 1),
        ],
        axis=1,
    )
    mask_rows = (slab_pos[:, None] == sub_pos[None, :]).astype(jnp.float32)
    mask_cols = (sub_pos[:, None] == slab_pos[None, :]).astype(jnp.float32)

    def one_turn(offset, visiting, carried):
        grad_left, grad_right, corr_parts, loss_part = carried
        owner = (wide_index - offset) % wide_size
        vis_a = visiting[:, :sub_cols]
        vis_b = visiting[:, sub_cols:]
        row_block = (
            lax.dot_general(full_a, vis_b, contract_rows, preferred_element_type=jnp.float32)
            / samples
        )
        col_block = (
            lax.dot_general(vis_a, full_b, contract_rows, preferred_element_type=jnp.float32)
            / samples
        )
        is_first = (jnp.asarray(offset) == 0).astype(jnp.float32)
        weight_rows = block_weights(row_block, mask_rows * is_first)
        weight_cols = block_weights(col_block, mask_cols * is_first)
        grad_left = grad_left + lax.dot_general(
            vis_b, weight_rows, contract_cols, preferred_element_type=jnp.float32
        )
        grad_right = grad_right + jnp.dot(vis_a, weight_cols, preferred_element_type=jnp.float32)
        corr_parts = lax.dynamic_update_slice(
            corr_parts, row_block.astype(jnp.bfloat16)[:, None, :], (0, owner, 0)
        )
        loss_part = loss_part + block_loss(row_block, mask_rows * is_first)
        return (grad_left, grad_right, corr_parts, loss_part)

    def loop_body(offset, state):
        visiting, carried = state
        carried = one_turn(offset, visiting, carried)
        visiting = from_behind(visiting, "wide", 1)
        return (visiting, carried)

    empty = jnp.zeros((samples, slab), jnp.float32)
    start = (empty, empty, jnp.zeros((slab, wide_size, sub_cols), jnp.bfloat16), jnp.float32(0.0))
    visiting, carried = lax.fori_loop(0, wide_size - 1, loop_body, (first_visit, start))
    grad_left, grad_right, corr_parts, loss_part = one_turn(wide_size - 1, visiting, carried)
    dstd = lax.psum_scatter(
        jnp.concatenate([grad_left, grad_right], axis=1).astype(jnp.bfloat16),
        "narrow",
        scatter_dimension=0,
        tiled=True,
    ).astype(jnp.float32)
    per_owner = narrow_size // wide_size
    target_pos = jnp.arange(narrow_size)
    owner_pos = jnp.arange(wide_size)
    selector = (
        target_pos[None, :] == owner_pos[:, None] * per_owner + narrow_index // wide_size
    ).astype(jnp.bfloat16)
    sendout = jnp.einsum(
        "iot,om->imt", corr_parts, selector, preferred_element_type=jnp.float32
    ).astype(jnp.bfloat16)
    received = lax.all_to_all(sendout, "narrow", split_axis=1, concat_axis=1, tiled=True)
    corr_local = lax.dynamic_slice_in_dim(
        received, narrow_index % per_owner * wide_size, wide_size, 1
    ).reshape(slab, wide_size * sub_cols)
    std_floats = arrived.astype(jnp.float32)
    moments = lax.psum(
        jnp.stack([jnp.sum(dstd, axis=0), jnp.sum(dstd * std_floats, axis=0)]), "narrow"
    )
    first_moment = moments[0] / samples
    second_moment = moments[1] / samples
    grads_home = (inv_own * (dstd - first_moment - std_floats * second_moment)).astype(jnp.bfloat16)
    loss_value = lax.psum(loss_part, ("wide", "narrow")) / features
    returned = lax.all_to_all(
        grads_home.reshape(quarter, 1, 2 * slab), "wide", split_axis=0, concat_axis=1, tiled=True
    )
    grad_a = returned[:, :, :slab].reshape(row_count, features)
    grad_b = returned[:, :, slab:].reshape(row_count, features)
    return (corr_local, loss_value, grad_a, grad_b)


def solution(mesh):
    return jax.shard_map(
        on_device,
        mesh=mesh,
        in_specs=(P(("wide", "narrow"), None), P(("wide", "narrow"), None)),
        out_specs=(
            P("wide", "narrow"),
            P(),
            P(("wide", "narrow"), None),
            P(("wide", "narrow"), None),
        ),
        check_vma=False,
    )
```

profile of v0, /device:TPU:0, one launch (start us, length us, event | category | flops | bytes accessed | tf_op | source)
XLA Modules:
  0.0 599.4 jit_solution(8243243232327923090)
XLA Ops:
  10.2 145.8 %all-reduce.2.cloned.1.call-done = f32[4,8192]{1,0:T(4,128)} async-done(((f32[4,8192]{1,0:T(4,128)}), f32[4,8192]{1,0:T(4,128)}) %all-reduce.2.cloned.1.call-update) | async-done | bytes 131088 | tf_op jit(solution)/shard_map/psum | solution.py:55
  159.1 10.7 %all_to_all.38 = bf16[8,8,2048]{2,0,1:T(8,128)(2,1)} all-to-all(bf16[8,8,2048]{2,0,1:T(8,128)(2,1)S(1)} %pad_maximum_fusion.1), channel_id=1, replica_groups=mesh['wide'=8,'narrow'=16] {'wide'}, dimensions={1} | all-to-all | bytes 524288 | tf_op jit(solution)/shard_map/all_to_all | solution.py:72
  170.0 48.4 %all-gather.2.cloned.1.call-done = bf16[1024,2048]{1,0:T(8,128)(2,1)} async-done(((bf16[64,2048]{1,0:T(8,128)(2,1)}), bf16[1024,2048]{1,0:T(8,128)(2,1)}) %all-gather.2.cloned.1.call-update) | async-done | bytes 4194320 | tf_op jit(solution)/shard_map/all_gather | solution.py:78
  219.8 4.0 fusion.98
  225.0 98.1 %while.27 = (s32[]{:T(128)}, bf16[1024,128]{1,0:T(8,128)(2,1)S(1)}, f32[1024,1024]{0,1:T(8,128)}, f32[1024,1024]{0,1:T(8,128)}, bf16[1024,8,64]{0,2,1:T(8,128)(2...) while((s32[]{:T(128)}, bf16[1024,128]{1,0:T(8,128)(2,1)S(1)}, ...), condition=%wide.region_7.8_spmd.clone.clone.clone, body=%wide.region_5.7_spmd.clone.clone.clone.sunk | while | flops 543162368 | bytes 24511864 | solution.py:127
  227.8 4.8 bitcast_add_fusion.5
  232.6 2.8 bitcast_add_fusion.4
  235.5 1.5 collective-permute-start
  239.8 6.0 %bitcast_add_fusion.5 = f32[1024,1024]{0,1:T(8,128)} fusion(f32[1024,1024]{0,1:T(8,128)} %get-tuple-element.553, pred[]{:T(512)S(6)} %compare.11, bf16[1024,128]{1,0:T(8,128)(2,1)S(1)} %copy.44, bf16[1024,1024]{1,0:T(8,128)(2,1)} %get-tuple-element.571, s32[64]{0:T(128)S(1)} %get-tuple-element.573, f32[]{:T(128)S(6)} %convert_element_type.198), kind=kOutput, calls=%fused_computation.2.clone.1 | convolution fusion | flops 271187968 | bytes 11010565 | tf_op jit(solution)/shard_map/while/body/eval_jaxpr/dot_general | solution.py:112
  245.9 5.0 bitcast_add_fusion.4
  253.7 6.0 %bitcast_add_fusion.5 = f32[1024,1024]{0,1:T(8,128)} fusion(f32[1024,1024]{0,1:T(8,128)} %get-tuple-element.553, pred[]{:T(512)S(6)} %compare.11, bf16[1024,128]{1,0:T(8,128)(2,1)S(1)} %copy.44, bf16[1024,1024]{1,0:T(8,128)(2,1)} %get-tuple-element.571, s32[64]{0:T(128)S(1)} %get-tuple-element.573, f32[]{:T(128)S(6)} %convert_element_type.198), kind=kOutput, calls=%fused_computation.2.clone.1 | convolution fusion | flops 271187968 | bytes 11010565 | tf_op jit(solution)/shard_map/while/body/eval_jaxpr/dot_general | solution.py:112
  259.8 5.0 bitcast_add_fusion.4
  264.8 1.5 collective-permute-start
  269.1 6.0 %bitcast_add_fusion.5 = f32[1024,1024]{0,1:T(8,128)} fusion(f32[1024,1024]{0,1:T(8,128)} %get-tuple-element.553, pred[]{:T(512)S(6)} %compare.11, bf16[1024,128]{1,0:T(8,128)(2,1)S(1)} %copy.44, bf16[1024,1024]{1,0:T(8,128)(2,1)} %get-tuple-element.571, s32[64]{0:T(128)S(1)} %get-tuple-element.573, f32[]{:T(128)S(6)} %convert_element_type.198), kind=kOutput, calls=%fused_computation.2.clone.1 | convolution fusion | flops 271187968 | bytes 11010565 | tf_op jit(solution)/shard_map/while/body/eval_jaxpr/dot_general | solution.py:112
  275.2 5.0 bitcast_add_fusion.4
  283.1 6.0 %bitcast_add_fusion.5 = f32[1024,1024]{0,1:T(8,128)} fusion(f32[1024,1024]{0,1:T(8,128)} %get-tuple-element.553, pred[]{:T(512)S(6)} %compare.11, bf16[1024,128]{1,0:T(8,128)(2,1)S(1)} %copy.44, bf16[1024,1024]{1,0:T(8,128)(2,1)} %get-tuple-element.571, s32[64]{0:T(128)S(1)} %get-tuple-element.573, f32[]{:T(128)S(6)} %convert_element_type.198), kind=kOutput, calls=%fused_computation.2.clone.1 | convolution fusion | flops 271187968 | bytes 11010565 | tf_op jit(solution)/shard_map/while/body/eval_jaxpr/dot_general | solution.py:112
  289.1 5.0 bitcast_add_fusion.4
  298.1 6.0 %bitcast_add_fusion.5 = f32[1024,1024]{0,1:T(8,128)} fusion(f32[1024,1024]{0,1:T(8,128)} %get-tuple-element.553, pred[]{:T(512)S(6)} %compare.11, bf16[1024,128]{1,0:T(8,128)(2,1)S(1)} %copy.44, bf16[1024,1024]{1,0:T(8,128)(2,1)} %get-tuple-element.571, s32[64]{0:T(128)S(1)} %get-tuple-element.573, f32[]{:T(128)S(6)} %convert_element_type.198), kind=kOutput, calls=%fused_computation.2.clone.1 | convolution fusion | flops 271187968 | bytes 11010565 | tf_op jit(solution)/shard_map/while/body/eval_jaxpr/dot_general | solution.py:112
  304.2 5.0 bitcast_add_fusion.4
  312.1 6.0 %bitcast_add_fusion.5 = f32[1024,1024]{0,1:T(8,128)} fusion(f32[1024,1024]{0,1:T(8,128)} %get-tuple-element.553, pred[]{:T(512)S(6)} %compare.11, bf16[1024,128]{1,0:T(8,128)(2,1)S(1)} %copy.44, bf16[1024,1024]{1,0:T(8,128)(2,1)} %get-tuple-element.571, s32[64]{0:T(128)S(1)} %get-tuple-element.573, f32[]{:T(128)S(6)} %convert_element_type.198), kind=kOutput, calls=%fused_computation.2.clone.1 | convolution fusion | flops 271187968 | bytes 11010565 | tf_op jit(solution)/shard_map/while/body/eval_jaxpr/dot_general | solution.py:112
  318.1 5.0 bitcast_add_fusion.4
  323.1 2.8 fusion.68
  325.9 4.4 add_convert_fusion.1
  330.3 4.0 add_convert_fusion
  334.3 4.0 pad_maximum_fusion
  338.3 6.5 %copy.24 = bf16[1024,2048]{1,0:T(8,128)(2,1)} copy(bf16[1024,2048]{0,1:T(8,128)(2,1)} %pad_maximum_fusion) | data formatting | bytes 8388608
  347.0 2.5 copy.20
  349.5 5.3 all-to-all-start.1
  354.8 86.4 %reduce-scatter.4.cloned.1.call-done = bf16[64,2048]{1,0:T(8,128)(2,1)} async-done(((bf16[1024,2048]{1,0:T(8,128)(2,1)}), bf16[64,2048]{1,0:T(8,128)(2,1)}) %reduce-scatter.4.cloned.1.call-update) | async-done | bytes 262160 | tf_op jit(solution)/shard_map/reduce_scatter | solution.py:129
  442.3 72.1 %psum.23 = f32[2,2048]{1,0:T(2,128)S(1)} all-reduce(f32[2,2048]{1,0:T(2,128)S(1)} %pad_maximum_fusion.4), channel_id=1, replica_groups=mesh['wide'=8,'narrow'=16] {'narrow'}, use_global_device_ids=true, to_apply=%region_13.14 | all-reduce | flops 4096 | bytes 32768 | tf_op jit(solution)/shard_map/psum | solution.py:149
  517.7 4.3 all-to-all-start.2
  523.3 65.1 %psum.22 = f32[]{:T(128)} all-reduce(f32[]{:T(128)S(6)} %add.194), channel_id=1, replica_groups=mesh['wide'=8,'narrow'=16] {'wide','narrow'}, use_global_device_ids=true, to_apply=%region_9.10 | all-reduce | flops 1 | bytes 8 | tf_op jit(solution)/shard_map/psum | solution.py:155
  (76 shorter events, 34.7 us)
Async XLA Ops:
  7.2 148.8 %all-reduce.2.cloned.1.call-start = ((), (), s32[]{:S(2)}) async-start(), calls=%async_computation.4 | async-start | bytes 262144 | tf_op jit(solution)/shard_map/psum | solution.py:55
  10.2 208.3 %all-gather.2.cloned.1.call-start = ((), (), s32[]{:S(2)}) async-start(), calls=%async_computation.5 | async-start | bytes 4456448 | tf_op jit(solution)/shard_map/all_gather | solution.py:78
  169.9 271.3 %reduce-scatter.4.cloned.1.call-start = ((), (), s32[]{:S(2)}) async-start(), calls=%async_computation.6 | async-start | bytes 4456448 | tf_op jit(solution)/shard_map/reduce_scatter | solution.py:129
  225.0 10.5 %collective-permute-start = (bf16[1024,128]{1,0:T(8,128)(2,1)S(1)}, bf16[1024,128]{1,0:T(8,128)(2,1)S(1)}, u32[]{:S(2)}, u32[]{:S(2)}) collective-permute-start(bf16[1024,128]{1,0:T(8,128)(2,1)S(1)} %copy.44), channel_id=1, source_target_pairs={{0,16},{16,32},{32,48},{48,64},{64,80},{80,96},{96,112},{112,0},{1... | collective-permute-start | bytes 786440 | tf_op jit(solution)/shard_map/while/body/eval_jaxpr/ppermute | solution.py:12
  235.5 15.4 %collective-permute-start = (bf16[1024,128]{1,0:T(8,128)(2,1)S(1)}, bf16[1024,128]{1,0:T(8,128)(2,1)S(1)}, u32[]{:S(2)}, u32[]{:S(2)}) collective-permute-start(bf16[1024,128]{1,0:T(8,128)(2,1)S(1)} %copy.44), channel_id=1, source_target_pairs={{0,16},{16,32},{32,48},{48,64},{64,80},{80,96},{96,112},{112,0},{1... | collective-permute-start | bytes 786440 | tf_op jit(solution)/shard_map/while/body/eval_jaxpr/ppermute | solution.py:12
  250.9 13.9 %collective-permute-start = (bf16[1024,128]{1,0:T(8,128)(2,1)S(1)}, bf16[1024,128]{1,0:T(8,128)(2,1)S(1)}, u32[]{:S(2)}, u32[]{:S(2)}) collective-permute-start(bf16[1024,128]{1,0:T(8,128)(2,1)S(1)} %copy.44), channel_id=1, source_target_pairs={{0,16},{16,32},{32,48},{48,64},{64,80},{80,96},{96,112},{112,0},{1... | collective-permute-start | bytes 786440 | tf_op jit(solution)/shard_map/while/body/eval_jaxpr/ppermute | solution.py:12
  264.8 15.4 %collective-permute-start = (bf16[1024,128]{1,0:T(8,128)(2,1)S(1)}, bf16[1024,128]{1,0:T(8,128)(2,1)S(1)}, u32[]{:S(2)}, u32[]{:S(2)}) collective-permute-start(bf16[1024,128]{1,0:T(8,128)(2,1)S(1)} %copy.44), channel_id=1, source_target_pairs={{0,16},{16,32},{32,48},{48,64},{64,80},{80,96},{96,112},{112,0},{1... | collective-permute-start | bytes 786440 | tf_op jit(solution)/shard_map/while/body/eval_jaxpr/ppermute | solution.py:12
  280.2 13.9 %collective-permute-start = (bf16[1024,128]{1,0:T(8,128)(2,1)S(1)}, bf16[1024,128]{1,0:T(8,128)(2,1)S(1)}, u32[]{:S(2)}, u32[]{:S(2)}) collective-permute-start(bf16[1024,128]{1,0:T(8,128)(2,1)S(1)} %copy.44), channel_id=1, source_target_pairs={{0,16},{16,32},{32,48},{48,64},{64,80},{80,96},{96,112},{112,0},{1... | collective-permute-start | bytes 786440 | tf_op jit(solution)/shard_map/while/body/eval_jaxpr/ppermute | solution.py:12
  294.1 15.1 %collective-permute-start = (bf16[1024,128]{1,0:T(8,128)(2,1)S(1)}, bf16[1024,128]{1,0:T(8,128)(2,1)S(1)}, u32[]{:S(2)}, u32[]{:S(2)}) collective-permute-start(bf16[1024,128]{1,0:T(8,128)(2,1)S(1)} %copy.44), channel_id=1, source_target_pairs={{0,16},{16,32},{32,48},{48,64},{64,80},{80,96},{96,112},{112,0},{1... | collective-permute-start | bytes 786440 | tf_op jit(solution)/shard_map/while/body/eval_jaxpr/ppermute | solution.py:12
  309.2 13.9 %collective-permute-start = (bf16[1024,128]{1,0:T(8,128)(2,1)S(1)}, bf16[1024,128]{1,0:T(8,128)(2,1)S(1)}, u32[]{:S(2)}, u32[]{:S(2)}) collective-permute-start(bf16[1024,128]{1,0:T(8,128)(2,1)S(1)} %copy.44), channel_id=1, source_target_pairs={{0,16},{16,32},{32,48},{48,64},{64,80},{80,96},{96,112},{112,0},{1... | collective-permute-start | bytes 786440 | tf_op jit(solution)/shard_map/while/body/eval_jaxpr/ppermute | solution.py:12
  344.8 1.2 copy-start.1
  347.0 94.2 %copy-start = (bf16[8,8,2048]{2,0,1:T(8,128)(2,1)S(1)}, bf16[8,8,2048]{2,0,1:T(8,128)(2,1)}, u32[]{:S(2)}) copy-start(bf16[8,8,2048]{2,0,1:T(8,128)(2,1)} %all_to_all.38) | copy-start | bytes 786436
  349.5 168.3 %all-to-all-start.1 = ((bf16[1024,16,64]{0,2,1:T(8,128)(2,1)}), bf16[1024,16,64]{0,2,1:T(8,128)(2,1)S(1)}, u32[]{:S(2)}, u32[]{:S(2)}) async-start(bf16[1024,16,64]{0,2,1:T(8,128)(2,1)} %copy.20), calls=%async_computation.1 | async-start | bytes 4194304 | tf_op jit(solution)/shard_map/all_to_all | solution.py:144
  517.7 72.8 %all-to-all-start.2 = ((bf16[8,2,8192]{2,1,0:T(2,128)(2,1)}), bf16[8,2,8192]{2,1,0:T(2,128)(2,1)S(1)}, u32[]{:S(2)}, u32[]{:S(2)}) async-start(bf16[8,2,8192]{2,1,0:T(2,128)(2,1)} %reshape.56), calls=%async_computation.2 | async-start | bytes 524288 | tf_op jit(solution)/shard_map/all_to_all | solution.py:156
Sparse Core Ops, SparseCore 0:
  13.3 142.6 all-reduce.1
  170.0 48.3 all-gather.1
  345.0 96.1 reduce-scatter.3
where the time goes:
time: 601 us; the launch traced here: 599 us
  waiting for transfers between devices  281 us (47%)
  blocking collectives  148 us (25%)
  matrix products  94.7 us (16%)
  local copies, waits for them, and re-layouts  20.8 us (3%)
  other arithmetic  19.6 us (3%)
  between operations  16.4 us (3%)
  starting transfers between devices  14.2 us (2%)
    psum x1, waiting for transfers between devices, on_device(): lax.psum(jnp.stack([jnp.sum(floats_a, axis=0), jnp.sum(floats_b, axis=0),...  146 us
    reduce_scatter x1, waiting for transfers between devices, on_device(): lax.psum_scatter(jnp.concatenate([grad_left, grad_right], axis=1).astype(...  86.4 us
    psum x1, blocking collectives, on_device(): lax.psum(jnp.stack([jnp.sum(dstd, axis=0), jnp.sum(dstd * std_floats, axi...  72.1 us
    psum x1, blocking collectives, on_device(): loss_value = lax.psum(loss_part, ('wide', 'narrow')) / features  65.1 us
    all_gather x1, waiting for transfers between devices, on_device(): full_slab = lax.all_gather(arrived, 'narrow', axis=0, tiled=True)  48.4 us
    dot_general x8, matrix products, one_turn(): jnp.dot(vis_a, weight_cols, preferred_element_type=jnp.float32)  45.1 us
    dot_general x8, matrix products, one_turn(): lax.dot_general(vis_b, weight_rows, contract_cols, preferred_element_type...  37.1 us
  transfers between devices with their start and end apart: 12, of which 3 were waited for; matrix products, arithmetic and copies ran while one was open for 16% of the time, Pallas kernels for 0%

commit v1 on v0

v1 whole, which is shorter than its diff:
```python
import functools

import jax
import jax.numpy as jnp
from jax import lax
from jax.experimental import pallas as pl
from jax.experimental.pallas import tpu as pltpu
from jax.sharding import PartitionSpec as P

off_weight = 0.0051
epsilon = 1e-05
MESH = pl.DeviceIdType.MESH
F32 = jnp.float32
BF16 = jnp.bfloat16


def kernel(
    WN, NN, BLK, SAMPLES,
    a_ref, b_ref,
    corr_ref, loss_ref, ga_ref, gb_ref,
    xa, xb, xb2, xa2,
    A3, B3, b1w, a1n,
    S_a, S_b, SR_a,
    gas, gar, gaall, gbs, gbr, gball,
    va, vb, Dn, Dw,
    dA, dB,
    mas, mar, mbs, mbr,
    ras, rar, rbs, rbr,
    lbuf, lsend, lrecv, corr_v,
    s_w, r_w, s_n, r_n, corr_sem,
):
    SLAB = BLK * (NN // WN)
    HB, HS = BLK // 2, SLAB // 2
    HN = SAMPLES // 2
    FEATS = BLK * NN
    w = lax.axis_index("wide")
    n = lax.axis_index("narrow")
    diag = lax.div(n, 2) == w

    def wide_copy(which, k, src, dst):
        return pltpu.make_async_remote_copy(
            src_ref=src, dst_ref=dst,
            send_sem=s_w.at[which, k], recv_sem=r_w.at[which, k],
            device_id=(lax.rem(w + k, WN), n), device_id_type=MESH,
        )

    def narrow_copy(which, k, src, dst):
        return pltpu.make_async_remote_copy(
            src_ref=src, dst_ref=dst,
            send_sem=s_n.at[which, k], recv_sem=r_n.at[which, k],
            device_id=(w, lax.rem(n + k, NN)), device_id_type=MESH,
        )

    def each(count, body):
        def step(k, c):
            body(k)
            return c
        lax.fori_loop(1, count, step, 0)

    def wide_a2a(which, src, dst):
        each(WN, lambda k: wide_copy(which, k, src.at[lax.rem(w + k, WN)], dst.at[w]).start())

    def narrow_a2a(which, src, dst):
        each(NN, lambda k: narrow_copy(which, k, src.at[lax.rem(n + k, NN)], dst.at[n]).start())

    def wide_bcast(which, src, dst):
        each(WN, lambda k: wide_copy(which, k, src, dst.at[w]).start())

    def narrow_bcast(which, src, dst):
        each(NN, lambda k: narrow_copy(which, k, src, dst.at[n]).start())

    def wide_recv(which, dst):
        each(WN, lambda k: wide_copy(which, k, dst.at[0], dst.at[0]).wait_recv())

    def narrow_recv(which, dst):
        each(NN, lambda k: narrow_copy(which, k, dst.at[0], dst.at[0]).wait_recv())

    def wide_sent(which, src):
        each(WN, lambda k: wide_copy(which, k, src, src).wait_send())

    def narrow_sent(which, src):
        each(NN, lambda k: narrow_copy(which, k, src, src).wait_send())

    barrier = pltpu.get_barrier_semaphore()
    each(WN, lambda k: pl.semaphore_signal(
        barrier, inc=1, device_id=(lax.rem(w + k, WN), n), device_id_type=MESH))
    each(NN, lambda k: pl.semaphore_signal(
        barrier, inc=1, device_id=(w, lax.rem(n + k, NN)), device_id_type=MESH))

    def stack(ref, base, half):
        return jnp.concatenate(
            [ref[:, base:base + half], ref[:, base + half:base + 2 * half]], axis=0)

    for i in range(WN):
        xa[i] = stack(a_ref, i * SLAB, HS)
    for i in range(NN):
        xb[i] = stack(b_ref, i * BLK, HB)
    pl.semaphore_wait(barrier, WN + NN - 2)

    wide_a2a(0, xa, A3.at[n])
    narrow_a2a(0, xb, B3.at[w])
    A3[n, w] = xa[w]
    B3[w, n] = xb[n]
    for i in range(WN):
        xb2[i] = stack(b_ref, i * SLAB, HS)
    for i in range(NN):
        xa2[i] = stack(a_ref, i * BLK, HB)
    b1w[w] = xb2[w]
    a1n[n] = xa2[n]
    wide_recv(0, A3.at[n])
    narrow_bcast(1, A3.at[n], A3)
    narrow_recv(0, B3.at[w])
    wide_bcast(1, B3.at[w], B3)
    wide_a2a(2, xb2, b1w)
    narrow_a2a(2, xa2, a1n)

    def add_sums(ref, sums):
        def step(i, c):
            v = ref[i].astype(F32)
            return (c[0] + v, c[1] + v * v)
        return lax.fori_loop(0, ref.shape[0], step, sums, unroll=4)

    def moments_of(sums):
        total, squares = sums

        def fold(t):
            return [jnp.sum(t[h * 8:(h + 1) * 8], axis=0, keepdims=True) / SAMPLES for h in (0, 1)]
        means, seconds = fold(total), fold(squares)
        invs = [lax.rsqrt(q - m * m + epsilon) for q, m in zip(seconds, means)]
        return means, invs

    def stacked(halves):
        return jnp.concatenate([jnp.broadcast_to(h, (8, h.shape[1])) for h in halves], axis=0)

    zero = jnp.zeros((16, HB), F32)
    sums = add_sums(B3.at[w], (zero, zero))

    def arrive_b(k, c):
        wide_copy(1, k, B3.at[0], B3.at[0]).wait_recv()
        return add_sums(B3.at[lax.rem(w - k + WN, WN)], c)
    sums = lax.fori_loop(1, WN, arrive_b, sums)
    mean_b, inv_b = moments_of(sums)
    mean2, inv2 = stacked(mean_b), stacked(inv_b)

    def norm_b(i, c):
        src, pair = lax.div(i, NN // 2), lax.rem(i, NN // 2)
        even = (B3[src, 2 * pair].astype(F32) - mean2) * inv2
        odd = (B3[src, 2 * pair + 1].astype(F32) - mean2) * inv2
        at = pl.ds(pl.multiple_of(i * 16, 16), 16)
        for h in (0, 1):
            S_b[at, h * HB:(h + 1) * HB] = jnp.concatenate(
                [even[h * 8:h * 8 + 8], odd[h * 8:h * 8 + 8]], axis=0).astype(BF16)
        return c
    lax.fori_loop(0, SAMPLES // 16, norm_b, 0, unroll=2)

    dot_last = functools.partial(
        lax.dot_general, dimension_numbers=(((1,), (1,)), ((), ())), preferred_element_type=F32)

    def stack_gram(dst, g):
        count = g.shape[0] // 8
        g3 = g.reshape(count, 8, SAMPLES)
        dst[...] = jnp.concatenate([g3[:, :, :HN], g3[:, :, HN:]], axis=1).astype(BF16)

    own_rows = S_b[pl.ds(pl.multiple_of(w * NN * 8, 16), NN * 8), :]
    stack_gram(gbs, dot_last(own_rows, S_b[...]))
    narrow_a2a(3, gbs, gbr)
    gbr[n] = gbs[n]

    zero = jnp.zeros((16, HS), F32)
    sums = add_sums(A3.at[n], (zero, zero))

    def arrive_a(k, c):
        narrow_copy(1, k, A3.at[0], A3.at[0]).wait_recv()
        return add_sums(A3.at[lax.rem(n - k + NN, NN)], c)
    sums = lax.fori_loop(1, NN, arrive_a, sums)
    mean_a, inv_a = moments_of(sums)
    mean2a, inv2a = stacked(mean_a), stacked(inv_a)

    def norm_a(i, c):
        src, pair = lax.div(i, NN // 2), lax.rem(i, NN // 2)
        even = (A3[2 * pair, src].astype(F32) - mean2a) * inv2a
        odd = (A3[2 * pair + 1, src].astype(F32) - mean2a) * inv2a
        at = pl.ds(pl.multiple_of(i * 16, 16), 16)
        for h in (0, 1):
            S_a[at, h * HS:(h + 1) * HS] = jnp.concatenate(
                [even[h * 8:h * 8 + 8], odd[h * 8:h * 8 + 8]], axis=0).astype(BF16)
        return c
    lax.fori_loop(0, SAMPLES // 16, norm_a, 0)
    for i in range(WN // 2):
        even = (A3[n, 2 * i].astype(F32) - mean2a) * inv2a
        odd = (A3[n, 2 * i + 1].astype(F32) - mean2a) * inv2a
        for h in (0, 1):
            SR_a[i * 16:i * 16 + 16, h * HS:(h + 1) * HS] = jnp.concatenate(
                [even[h * 8:h * 8 + 8], odd[h * 8:h * 8 + 8]], axis=0).astype(BF16)

    stack_gram(gas, dot_last(SR_a[...], S_a[...]))
    wide_a2a(3, gas, gar)
    gar[w] = gas[w]

    half = lax.rem(n, 2)
    lbuf[...] = jnp.zeros_like(lbuf)

    @pl.when(diag)
    def _():
        def step(i, c):
            at = pl.ds(pl.multiple_of(i * 16, 16), 16)
            cols = pl.ds(pl.multiple_of(half * BLK, BLK), BLK)
            return c + S_a[at, cols].astype(F32) * S_b[at, :].astype(F32)
        prod = lax.fori_loop(0, SAMPLES // 16, step, jnp.zeros((16, BLK), F32), unroll=4)
        c = jnp.sum(prod, axis=0, keepdims=True) / SAMPLES
        d = -2.0 * (1.0 - c) - 2.0 * off_weight * c
        mb = jnp.concatenate(mean_b, axis=1)
        ib = jnp.concatenate(inv_b, axis=1)
        first = (half == 0).astype(F32)
        ma = mean_a[0] * first + mean_a[1] * (1.0 - first)
        ia = inv_a[0] * first + inv_a[1] * (1.0 - first)
        pad = jnp.zeros((5, BLK), F32)
        va[...] = jnp.concatenate([ma, ia, d, pad], axis=0)
        vb[...] = jnp.concatenate([mb, ib, d, pad], axis=0)
        Dn[...] = va[...]
        Dw[half] = vb[...]
        lbuf[0:1, :] = (1.0 - c) * (1.0 - c) - off_weight * c * c
        each(WN, lambda k: wide_copy(4, k, va, Dn).start())
        each(NN, lambda k: narrow_copy(4, k, vb, Dw.at[half]).start())

    narrow_recv(3, gbr)

    def total_of(ref):
        t = ref[0].astype(F32)
        for i in range(1, ref.shape[0]):
            t = t + ref[i].astype(F32)
        return t
    gball[w] = total_of(gbr).astype(BF16)
    wide_bcast(5, gball.at[w], gball)

    TM = 256 if SLAB % 256 == 0 else SLAB

    def corr_out(i):
        at = pl.ds(pl.multiple_of(i * TM, TM), TM)
        return pltpu.make_async_copy(corr_v.at[at, :], corr_ref.at[at, :], corr_sem.at[i])

    def cross_tile(i, acc):
        at = pl.ds(pl.multiple_of(i * TM, TM), TM)
        c = lax.dot_general(
            S_a[:, at], S_b[...], (((0,), (0,)), ((), ())), preferred_element_type=F32
        ) * (1.0 / SAMPLES)
        corr_v[at, :] = c.astype(BF16)
        corr_out(i).start()
        return acc + jnp.sum((c * c).reshape(TM // 8, 8, BLK), axis=0)
    tiles = SLAB // TM
    acc = lax.fori_loop(0, 1, cross_tile, jnp.zeros((8, BLK), F32))

    wide_recv(3, gar)
    gaall[n] = total_of(gar).astype(BF16)
    narrow_bcast(5, gaall.at[n], gaall)
    acc = lax.fori_loop(1, tiles, cross_tile, acc)
    lbuf[...] = lbuf[...] + off_weight * acc

    wide_recv(2, b1w)
    narrow_recv(2, a1n)

    @pl.when(lax.div(n, 2) != w)
    def _():
        wide_copy(4, lax.rem(w - lax.div(n, 2) + WN, WN), va, Dn).wait_recv()
    for h in (0, 1):
        @pl.when(n != 2 * w + h)
        def _():
            narrow_copy(4, lax.rem(n - 2 * w - h + NN, NN), vb, Dw.at[h]).wait_recv()

    vec = lambda r, i: [Dw[h, i:i + 1, :] for h in (0, 1)]
    dmean, dinv, dd = (stacked([Dw[h, i:i + 1, :] for h in (0, 1)]) for i in range(3))
    for i in range(WN):
        s = ((b1w[i].astype(F32) - dmean) * dinv).astype(BF16).astype(F32) * dd
        for h in (0, 1):
            dA[i * 8:i * 8 + 8, h * HS:(h + 1) * HS] = s[h * 8:h * 8 + 8]
    dmean, dinv, dd = (
        stacked([Dn[i:i + 1, h * HB:(h + 1) * HB] for h in (0, 1)]) for i in range(3))
    for i in range(NN):
        s = ((a1n[i].astype(F32) - dmean) * dinv).astype(BF16).astype(F32) * dd
        for h in (0, 1):
            dB[i * 8:i * 8 + 8, h * HB:(h + 1) * HB] = s[h * 8:h * 8 + 8]

    factor = 2.0 * off_weight / SAMPLES

    def unstack(ref):
        g = ref[...].astype(F32)
        rows = ref.shape[0] * 8
        return [g[:, h * 8:h * 8 + 8, :].reshape(rows, HN).astype(BF16) for h in (0, 1)]

    def sum_messages(ref):
        t = ref[0]
        for i in range(1, ref.shape[0]):
            t = t + ref[i]
        return t

    wide_recv(5, gball)
    g0, g1 = unstack(gball)
    Q = SLAB // 4
    d = factor * (
        jnp.dot(g0, S_a[:HN, :], preferred_element_type=F32)
        + jnp.dot(g1, S_a[HN:, :], preferred_element_type=F32)
    ) + dA[...]
    dA[...] = d
    m1 = jnp.sum(d, axis=0, keepdims=True)
    m2 = jnp.sum(d * SR_a[...].astype(F32), axis=0, keepdims=True)
    mas[0:8, :] = jnp.concatenate(
        [m[:, q * Q:(q + 1) * Q] for m in (m1, m2) for q in range(4)], axis=0)
    mas[8:16, :] = lbuf[:, :BLK // 2] + lbuf[:, BLK // 2:]
    narrow_bcast(6, mas, mar)
    mar[n] = mas[...]

    narrow_recv(5, gaall)
    g0, g1 = unstack(gaall)
    own = pl.ds(pl.multiple_of(w * NN * 8, 16), NN * 8)
    d = factor * (
        jnp.dot(g0, S_b[:HN, :], preferred_element_type=F32)
        + jnp.dot(g1, S_b[HN:, :], preferred_element_type=F32)
    ) + dB[...]
    dB[...] = d
    m1 = jnp.sum(d, axis=0, keepdims=True)
    m2 = jnp.sum(d * S_b[own, :].astype(F32), axis=0, keepdims=True)
    QB = BLK // 4
    mbs[...] = jnp.concatenate(
        [m[:, q * QB:(q + 1) * QB] for m in (m1, m2) for q in range(4)], axis=0)
    wide_bcast(6, mbs, mbr)
    mbr[w] = mbs[...]

    narrow_recv(6, mar)
    total = sum_messages(mar) / SAMPLES
    m1 = jnp.concatenate([total[q:q + 1] for q in range(4)], axis=1)
    m2 = jnp.concatenate([total[q + 4:q + 5] for q in range(4)], axis=1)
    inv = jnp.concatenate(inv_a, axis=1)
    grad = inv * (dA[...] - m1 - SR_a[...].astype(F32) * m2)
    for i in range(WN):
        ras[i] = jnp.concatenate(
            [grad[i * 8:i * 8 + 8, h * HS:(h + 1) * HS] for h in (0, 1)], axis=0).astype(BF16)
    wide_a2a(7, ras, rar)
    rar[w] = ras[w]
    lsend[...] = total[8:16] * SAMPLES
    wide_bcast(8, lsend, lrecv)
    lrecv[w] = lsend[...]

    wide_recv(6, mbr)
    total = sum_messages(mbr) / SAMPLES
    m1 = jnp.concatenate([total[q:q + 1] for q in range(4)], axis=1)
    m2 = jnp.concatenate([total[q + 4:q + 5] for q in range(4)], axis=1)
    inv = jnp.concatenate(inv_b, axis=1)
    grad = inv * (dB[...] - m1 - S_b[own, :].astype(F32) * m2)
    for i in range(NN):
        rbs[i] = jnp.concatenate(
            [grad[i * 8:i * 8 + 8, h * HB:(h + 1) * HB] for h in (0, 1)], axis=0).astype(BF16)
    narrow_a2a(7, rbs, rbr)
    rbr[n] = rbs[n]

    wide_recv(7, rar)
    for i in range(WN):
        for h in (0, 1):
            ga_ref[:, i * SLAB + h * HS:i * SLAB + (h + 1) * HS] = rar[i, h * 8:h * 8 + 8, :]
    wide_recv(8, lrecv)
    loss = jnp.sum(sum_messages(lrecv), keepdims=True) / FEATS
    loss_ref[...] = jnp.broadcast_to(loss, loss_ref.shape)
    narrow_recv(7, rbr)
    for i in range(NN):
        for h in (0, 1):
            gb_ref[:, i * BLK + h * HB:i * BLK + (h + 1) * HB] = rbr[i, h * 8:h * 8 + 8, :]

    wide_sent(0, xa.at[0])
    narrow_sent(0, xb.at[0])
    wide_sent(1, B3.at[0])
    narrow_sent(1, A3.at[0])
    wide_sent(2, xb2.at[0])
    narrow_sent(2, xa2.at[0])
    wide_sent(3, gas.at[0])
    narrow_sent(3, gbs.at[0])

    @pl.when(diag)
    def _():
        wide_sent(4, va)
        narrow_sent(4, vb)
    wide_sent(5, gball.at[0])
    narrow_sent(5, gaall.at[0])
    wide_sent(6, mbs)
    narrow_sent(6, mas)
    wide_sent(7, ras.at[0])
    narrow_sent(7, rbs.at[0])
    wide_sent(8, lsend)
    lax.fori_loop(0, tiles, lambda i, c: (corr_out(i).wait(), c)[1], 0)


def solution(mesh):
    WN, NN = mesh.shape["wide"], mesh.shape["narrow"]

    def on_device(view_a, view_b):
        rows, features = view_a.shape
        samples = rows * WN * NN
        BLK = features // NN
        SLAB = features // WN
        HB, HS, HN = BLK // 2, SLAB // 2, samples // 2
        V = pltpu.VMEM
        vmem = pl.BlockSpec(memory_space=pltpu.VMEM)
        corr, loss, ga, gb = pl.pallas_call(
            functools.partial(kernel, WN, NN, BLK, samples),
            out_shape=(
                jax.ShapeDtypeStruct((SLAB, BLK), BF16),
                jax.ShapeDtypeStruct((8, 128), F32),
                jax.ShapeDtypeStruct((rows, features), BF16),
                jax.ShapeDtypeStruct((rows, features), BF16),
            ),
            in_specs=[vmem, vmem],
            out_specs=(pl.BlockSpec(memory_space=pl.ANY), vmem, vmem, vmem),
            scratch_shapes=[
                V((WN, 16, HS), BF16), V((NN, 16, HB), BF16),
                V((WN, 16, HS), BF16), V((NN, 16, HB), BF16),
                V((NN, WN, 16, HS), BF16), V((WN, NN, 16, HB), BF16),
                V((WN, 16, HS), BF16), V((NN, 16, HB), BF16),
                V((samples, SLAB), BF16), V((samples, BLK), BF16), V((WN * 8, SLAB), BF16),
                V((WN, 16, HN), BF16), V((WN, 16, HN), BF16), V((NN, 16, HN), BF16),
                V((NN, 16, HN), BF16), V((NN, 16, HN), BF16), V((WN, 16, HN), BF16),
                V((8, BLK), F32), V((8, BLK), F32), V((8, BLK), F32), V((2, 8, BLK), F32),
                V((WN * 8, SLAB), F32), V((NN * 8, BLK), F32),
                V((16, SLAB // 4), F32), V((NN, 16, SLAB // 4), F32),
                V((8, BLK // 4), F32), V((WN, 8, BLK // 4), F32),
                V((WN, 16, HS), BF16), V((WN, 16, HS), BF16),
                V((NN, 16, HB), BF16), V((NN, 16, HB), BF16),
                V((8, BLK), F32), V((8, BLK // 2), F32), V((WN, 8, BLK // 2), F32),
                V((SLAB, BLK), BF16),
                pltpu.SemaphoreType.DMA((9, WN)), pltpu.SemaphoreType.DMA((9, WN)),
                pltpu.SemaphoreType.DMA((9, NN)), pltpu.SemaphoreType.DMA((9, NN)),
                pltpu.SemaphoreType.DMA((8,)),
            ],
            compiler_params=pltpu.CompilerParams(
                collective_id=0, has_side_effects=True, vmem_limit_bytes=56 * 1024 * 1024),
        )(view_a, view_b)
        return corr, loss[0, 0], ga, gb

    return jax.shard_map(
        on_device,
        mesh=mesh,
        in_specs=(P(("wide", "narrow"), None), P(("wide", "narrow"), None)),
        out_specs=(
            P("wide", "narrow"),
            P(),
            P(("wide", "narrow"), None),
            P(("wide", "narrow"), None),
        ),
        check_vma=False,
    )
```

time: 601 us -> 79.4 us (0.13)
  waiting for transfers between devices: 281 us -> 0 us
  blocking collectives: 148 us -> 0 us
  matrix products: 94.7 us -> 0 us
  Pallas kernels: 0 us -> 73.5 us
  other arithmetic: 19.6 us -> 0 us
  between operations: 16.4 us -> 0.64 us
  local copies, waits for them, and re-layouts: 20.8 us -> 5.1 us
  starting transfers between devices: 14.2 us -> 0 us
    psum x1 -> x0, waiting for transfers between devices: 146 us -> none  [on_device(): lax.psum(jnp.stack([jnp.sum(floats_a, axis=0), jnp.sum(floats_b, axis=0),...]
    psum x2 -> x0, blocking collectives: 137 us -> none  [the longest x1 72.1 us: on_device(): lax.psum(jnp.stack([jnp.sum(dstd, axis=0), jnp.sum(dstd * std_floats, axi...]
    dot_general x25 -> x0, matrix products: 94.7 us -> none  [the longest x8 45.1 us: one_turn(): jnp.dot(vis_a, weight_cols, preferred_element_type=jnp.float32)]
    reduce_scatter x1 -> x0, waiting for transfers between devices: 86.4 us -> none  [on_device(): lax.psum_scatter(jnp.concatenate([grad_left, grad_right], axis=1).astype(...]
    pallas_call x0 -> x1, Pallas kernels: none -> 73.5 us  [on_device(): pl.pallas_call(functools.partial(kernel, WN, NN, BLK, samples), out_shape...]
    all_gather x1 -> x0, waiting for transfers between devices: 48.4 us -> none  [on_device(): full_slab = lax.all_gather(arrived, 'narrow', axis=0, tiled=True)]
    all_to_all x1 -> x0, blocking collectives: 10.7 us -> none  [on_device(): lax.all_to_all(outgoing, 'wide', split_axis=1, concat_axis=0, tiled=True)]
    reduce_sum x11 -> x0, other arithmetic: 9.82 us -> none  [the longest x8 6.62 us: block_loss(): jnp.sum(jnp.where(diag_mask > 0.5, (1.0 - cross_corr) * (1.0 - cross_corr...]
  transfers between devices with their start and end apart: 12 -> 0, of which waited for: 3 -> 0; matrix products, arithmetic and copies ran while one was open for 16% -> 0% of each run, Pallas kernels for 0% -> 0%
where the time goes in v1:
time: 79.4 us; the launch traced here: 79.2 us
  Pallas kernels  73.5 us (93%)
  local copies, waits for them, and re-layouts  5.1 us (6%)
    pallas_call x1, Pallas kernels, on_device(): pl.pallas_call(functools.partial(kernel, WN, NN, BLK, samples), out_shape...  73.5 us
    unnamed x7, local copies, waits for them, and re-layouts  3.91 us

profile of v1, /device:TPU:0, one launch (start us, length us, event | category | flops | bytes accessed | tf_op | source)
XLA Modules:
  0.0 79.2 jit_solution(13164548575773680364)
XLA Ops:
  0.6 73.5 %shard_map.57 = (bf16[1024,512]{1,0:T(8,128)(2,1)}, f32[8,128]{1,0:T(8,128)}, bf16[8,8192]{1,0:T(8,128)(2,1)}, bf16[8,8192]{1,0:T(8,128)(2,1)}) custom-call(bf16[8,8192]{1,0:T(8,128)(2,1)} %a_ref.1, bf16[8,8192]{1,0:T(8,128)(2,1)} %b_ref.1), custom_call_target="tpu_custom_call" | custom-call | tf_op jit(solution)/shard_map/pallas_call | solution.py:401
  74.1 1.2 %slice.3 = f32[1,1]{1,0:T(1,128)} slice(f32[8,128]{1,0:T(8,128)} %get-tuple-element.9), slice={[0:1], [0:1]} | slice | bytes 8 | tf_op jit(solution)/shard_map/slice | solution.py:434
  75.3 0.0 copy-start.1
  75.3 2.3 %copy.9 = bf16[1024,512]{1,0:T(8,128)(2,1)} copy(bf16[1024,512]{1,0:T(8,128)(2,1)} %get-tuple-element.16) | data formatting | bytes 2097152
  77.6 0.0 copy-done.1
  77.6 0.0 copy-start
  77.6 0.7 copy.10
  78.3 0.3 copy-done
  78.5 0.7 copy.11
Async XLA Ops:
  75.3 2.3 %copy-start.1 = (bf16[8,8192]{1,0:T(8,128)(2,1)S(1)}, bf16[8,8192]{1,0:T(8,128)(2,1)}, u32[]{:S(2)}) copy-start(bf16[8,8192]{1,0:T(8,128)(2,1)} %get-tuple-element.18) | copy-start | bytes 393220
  77.6 1.0 %copy-start = (bf16[8,8192]{1,0:T(8,128)(2,1)S(1)}, bf16[8,8192]{1,0:T(8,128)(2,1)}, u32[]{:S(2)}) copy-start(bf16[8,8192]{1,0:T(8,128)(2,1)} %get-tuple-element.19) | copy-start | bytes 393220

commit v2 on v1

--- a/solution.py
+++ b/solution.py
@@ -16,8 +16,9 @@
 
 def kernel(
     WN, NN, BLK, SAMPLES,
-    a_ref, b_ref,
+    a_hbm, b_hbm,
     corr_ref, loss_ref, ga_ref, gb_ref,
+    a_ref, b_ref, dummy,
     xa, xb, xb2, xa2,
     A3, B3, b1w, a1n,
     S_a, S_b, SR_a,
@@ -26,8 +27,8 @@
     dA, dB,
     mas, mar, mbs, mbr,
     ras, rar, rbs, rbr,
-    lbuf, lsend, lrecv, corr_v,
-    s_w, r_w, s_n, r_n, corr_sem,
+    lbuf, lsend, lrecv,
+    s_w, r_w, s_n, r_n, r_a, r_b, r_d, in_sem,
 ):
     SLAB = BLK * (NN // WN)
     HB, HS = BLK // 2, SLAB // 2
@@ -39,15 +40,13 @@
 
     def wide_copy(which, k, src, dst):
         return pltpu.make_async_remote_copy(
-            src_ref=src, dst_ref=dst,
-            send_sem=s_w.at[which, k], recv_sem=r_w.at[which, k],
+            src_ref=src, dst_ref=dst, send_sem=s_w.at[which], recv_sem=r_w.at[which],
             device_id=(lax.rem(w + k, WN), n), device_id_type=MESH,
         )
 
     def narrow_copy(which, k, src, dst):
         return pltpu.make_async_remote_copy(
-            src_ref=src, dst_ref=dst,
-            send_sem=s_n.at[which, k], recv_sem=r_n.at[which, k],
+            src_ref=src, dst_ref=dst, send_sem=s_n.at[which], recv_sem=r_n.at[which],
             device_id=(w, lax.rem(n + k, NN)), device_id_type=MESH,
         )
 
@@ -57,6 +56,23 @@
             return c
         lax.fori_loop(1, count, step, 0)
 
+
+    def wide_recv(which, dst):
+        ref = dst.at[pl.ds(0, WN - 1)]
+        wide_copy(which, 1, ref, ref).wait_recv()
+
+    def narrow_recv(which, dst):
+        ref = dst.at[pl.ds(0, NN - 1)]
+        narrow_copy(which, 1, ref, ref).wait_recv()
+
+    def wide_sent(which, dst):
+        ref = dst.at[pl.ds(0, WN - 1)]
+        wide_copy(which, 1, ref, ref).wait_send()
+
+    def narrow_sent(which, dst):
+        ref = dst.at[pl.ds(0, NN - 1)]
+        narrow_copy(which, 1, ref, ref).wait_send()
+
     def wide_a2a(which, src, dst):
         each(WN, lambda k: wide_copy(which, k, src.at[lax.rem(w + k, WN)], dst.at[w]).start())
 
@@ -69,23 +85,20 @@
     def narrow_bcast(which, src, dst):
         each(NN, lambda k: narrow_copy(which, k, src, dst.at[n]).start())
 
-    def wide_recv(which, dst):
-        each(WN, lambda k: wide_copy(which, k, dst.at[0], dst.at[0]).wait_recv())
-
-    def narrow_recv(which, dst):
-        each(NN, lambda k: narrow_copy(which, k, dst.at[0], dst.at[0]).wait_recv())
-
-    def wide_sent(which, src):
-        each(WN, lambda k: wide_copy(which, k, src, src).wait_send())
-
-    def narrow_sent(which, src):
-        each(NN, lambda k: narrow_copy(which, k, src, src).wait_send())
-
+    loads = [
+        pltpu.make_async_copy(a_hbm, a_ref, in_sem.at[0]),
+        pltpu.make_async_copy(b_hbm, b_ref, in_sem.at[1]),
+    ]
+    for load in loads:
+        load.start()
     barrier = pltpu.get_barrier_semaphore()
     each(WN, lambda k: pl.semaphore_signal(
         barrier, inc=1, device_id=(lax.rem(w + k, WN), n), device_id_type=MESH))
     each(NN, lambda k: pl.semaphore_signal(
         barrier, inc=1, device_id=(w, lax.rem(n + k, NN)), device_id_type=MESH))
+
+    for load in loads:
+        load.wait()
 
     def stack(ref, base, half):
         return jnp.concatenate(
@@ -107,18 +120,71 @@
         xa2[i] = stack(a_ref, i * BLK, HB)
     b1w[w] = xb2[w]
     a1n[n] = xa2[n]
+    z, y = lax.div(n, 4), lax.rem(n, 4)
+    x, core = lax.div(w, 2), lax.rem(w, 2)
+    PART = WN // 2
+    FULL, FIRST, SECOND = (0, PART), (0, PART // 2), (PART // 2, PART // 2)
+
+    def slot(part, p, q):
+        dz, dy = (q, p) if part == 0 else (p, q)
+        return lax.rem(z + dz + 4, 4) * 4 + lax.rem(y + dy + 4, 4)
+
+    def piece(part, at, cut):
+        return A3.at[at, pl.ds(part * PART + cut[0], cut[1])]
+
+    def move(part, index, at, cut, p, q):
+        ref = piece(part, at, cut)
+        return pltpu.make_async_remote_copy(
+            src_ref=ref, dst_ref=ref, send_sem=s_n.at[1], recv_sem=r_a.at[part, index],
+            device_id=(w, slot(part, p, q)), device_id_type=MESH,
+        )
+
+    LINES = (0, -1, 1, 2)
+
+    def along(part, line, p, stage):
+        step = (lambda d: (d, 0)) if stage == 1 else (lambda d: (0, d))
+        for d, index in ((1, 0), (-1, 1)):
+            move(part, line * 4 + index, slot(part, p, 0), FULL, *step(d)).start()
+
+    def relay(part, line, p, stage):
+        for d, index, cut in ((1, 2, FIRST), (-1, 3, SECOND)):
+            got = slot(part, -d, 0) if stage == 1 else slot(part, p, -d)
+            step = (d, 0) if stage == 1 else (0, d)
+            move(part, line * 4 + index - 2, got, FULL, 0, 0).wait_recv()
+            move(part, line * 4 + index, got, cut, *step).start()
+
+    def far(part, line, p, stage):
+        got = slot(part, 2, 0) if stage == 1 else slot(part, p, 2)
+        for index, cut in ((2, FIRST), (3, SECOND)):
+            move(part, line * 4 + index, got, cut, 0, 0).wait_recv()
+
+    def move_b(index, at, dx, other):
+        ref = B3.at[at]
+        to = lax.rem(x + dx + 4, 4) * 2 + (1 - core if other else core)
+        return pltpu.make_async_remote_copy(
+            src_ref=ref, dst_ref=ref, send_sem=s_w.at[1], recv_sem=r_b.at[index],
+            device_id=(to, n), device_id_type=MESH,
+        )
+
+    def slot_b(dx, other):
+        return lax.rem(x + dx + 4, 4) * 2 + (1 - core if other else core)
+
     wide_recv(0, A3.at[n])
-    narrow_bcast(1, A3.at[n], A3)
+    for part in (0, 1):
+        along(part, 4, 0, 1)
+    for part in (0, 1):
+        along(part, 0, 0, 2)
     narrow_recv(0, B3.at[w])
-    wide_bcast(1, B3.at[w], B3)
+    for i, dx in enumerate((1, -1, 2)):
+        move_b(i, w, dx, False).start()
+    move_b(3, w, 0, True).start()
     wide_a2a(2, xb2, b1w)
-    narrow_a2a(2, xa2, a1n)
 
     def add_sums(ref, sums):
         def step(i, c):
             v = ref[i].astype(F32)
             return (c[0] + v, c[1] + v * v)
-        return lax.fori_loop(0, ref.shape[0], step, sums, unroll=4)
+        return lax.fori_loop(0, ref.shape[0], step, sums, unroll=min(4, ref.shape[0]))
 
     def moments_of(sums):
         total, squares = sums
@@ -132,14 +198,50 @@
     def stacked(halves):
         return jnp.concatenate([jnp.broadcast_to(h, (8, h.shape[1])) for h in halves], axis=0)
 
-    zero = jnp.zeros((16, HB), F32)
-    sums = add_sums(B3.at[w], (zero, zero))
-
-    def arrive_b(k, c):
-        wide_copy(1, k, B3.at[0], B3.at[0]).wait_recv()
-        return add_sums(B3.at[lax.rem(w - k + WN, WN)], c)
-    sums = lax.fori_loop(1, WN, arrive_b, sums)
-    mean_b, inv_b = moments_of(sums)
+    zero_b, zero_a = jnp.zeros((16, HB), F32), jnp.zeros((16, HS), F32)
+    sums_b = add_sums(B3.at[w], (zero_b, zero_b))
+    sums_a = add_sums(A3.at[n], (zero_a, zero_a))
+    for part in (0, 1):
+        relay(part, 4, 0, 1)
+    for part in (0, 1):
+        for line in (1, 2):
+            along(part, line, LINES[line], 2)
+
+    def take_b(i, dx, sums):
+        got = slot_b(-dx, False)
+        move_b(i, got, 0, False).wait_recv()
+        move_b(4 + i, got, 0, True).start()
+        return add_sums(B3.at[got], sums)
+
+    def sums_of_piece(part, at, sums):
+        return add_sums(piece(part, at, FULL), sums)
+
+    for part in (0, 1):
+        for p in (-1, 1):
+            sums_a = sums_of_piece(part, slot(part, p, 0), sums_a)
+    for part in (0, 1):
+        relay(part, 0, 0, 2)
+    for part in (0, 1):
+        far(part, 4, 0, 1)
+        along(part, 3, 2, 2)
+    for i, dx in ((0, 1), (1, -1)):
+        sums_b = take_b(i, dx, sums_b)
+    for part in (0, 1):
+        for line in (1, 2):
+            relay(part, line, LINES[line], 2)
+    sums_b = take_b(2, 2, sums_b)
+    for part in (0, 1):
+        for q in (-1, 1):
+            sums_a = sums_of_piece(part, slot(part, 0, q), sums_a)
+            for p in (-1, 1):
+                sums_a = sums_of_piece(part, slot(part, p, q), sums_a)
+        sums_a = sums_of_piece(part, slot(part, 2, 0), sums_a)
+    for i, dx in ((3, 0), (4, 1), (5, -1), (6, 2)):
+        move_b(i, slot_b(-dx, True), 0, True).wait_recv()
+        sums_b = add_sums(B3.at[slot_b(-dx, True)], sums_b)
+    for part in (0, 1):
+        relay(part, 3, 2, 2)
+    mean_b, inv_b = moments_of(sums_b)
     mean2, inv2 = stacked(mean_b), stacked(inv_b)
 
     def norm_b(i, c):
@@ -166,14 +268,15 @@
     narrow_a2a(3, gbs, gbr)
     gbr[n] = gbs[n]
 
-    zero = jnp.zeros((16, HS), F32)
-    sums = add_sums(A3.at[n], (zero, zero))
-
-    def arrive_a(k, c):
-        narrow_copy(1, k, A3.at[0], A3.at[0]).wait_recv()
-        return add_sums(A3.at[lax.rem(n - k + NN, NN)], c)
-    sums = lax.fori_loop(1, NN, arrive_a, sums)
-    mean_a, inv_a = moments_of(sums)
+    for part in (0, 1):
+        for q in (-1, 1):
+            sums_a = sums_of_piece(part, slot(part, 2, q), sums_a)
+    for line in range(4):
+        for part in (0, 1):
+            far(part, line, LINES[line], 2)
+            sums_a = sums_of_piece(part, slot(part, LINES[line], 2), sums_a)
+    narrow_a2a(2, xa2, a1n)
+    mean_a, inv_a = moments_of(sums_a)
     mean2a, inv2a = stacked(mean_a), stacked(inv_a)
 
     def norm_a(i, c):
@@ -199,6 +302,13 @@
 
     half = lax.rem(n, 2)
     lbuf[...] = jnp.zeros_like(lbuf)
+
+    def narrow_vec(k, h=None):
+        h = half if h is None else h
+        return pltpu.make_async_remote_copy(
+            src_ref=vb, dst_ref=Dw.at[h], send_sem=s_n.at[4], recv_sem=r_d.at[h],
+            device_id=(w, lax.rem(n + k, NN)), device_id_type=MESH,
+        )
 
     @pl.when(diag)
     def _():
@@ -221,7 +331,24 @@
         Dw[half] = vb[...]
         lbuf[0:1, :] = (1.0 - c) * (1.0 - c) - off_weight * c * c
         each(WN, lambda k: wide_copy(4, k, va, Dn).start())
-        each(NN, lambda k: narrow_copy(4, k, vb, Dw.at[half]).start())
+        each(NN, lambda k: narrow_vec(k).start())
+
+    def diag_recv():
+        @pl.when(lax.div(n, 2) != w)
+        def _():
+            wide_copy(4, 1, va, Dn).wait_recv()
+        for h in (0, 1):
+            @pl.when(n != 2 * w + h)
+            def _():
+                narrow_vec(1, h).wait_recv()
+
+    def diag_sent():
+        @pl.when(diag)
+        def _():
+            ref = dummy.at[pl.ds(0, WN - 1)]
+            wide_copy(4, 1, ref, ref).wait_send()
+            ref = dummy.at[pl.ds(0, NN - 1)]
+            narrow_copy(4, 1, ref, ref).wait_send()
 
     narrow_recv(3, gbr)
 
@@ -235,17 +362,12 @@
 
     TM = 256 if SLAB % 256 == 0 else SLAB
 
-    def corr_out(i):
-        at = pl.ds(pl.multiple_of(i * TM, TM), TM)
-        return pltpu.make_async_copy(corr_v.at[at, :], corr_ref.at[at, :], corr_sem.at[i])
-
     def cross_tile(i, acc):
         at = pl.ds(pl.multiple_of(i * TM, TM), TM)
         c = lax.dot_general(
             S_a[:, at], S_b[...], (((0,), (0,)), ((), ())), preferred_element_type=F32
         ) * (1.0 / SAMPLES)
-        corr_v[at, :] = c.astype(BF16)
-        corr_out(i).start()
+        corr_ref[at, :] = c.astype(BF16)
         return acc + jnp.sum((c * c).reshape(TM // 8, 8, BLK), axis=0)
     tiles = SLAB // TM
     acc = lax.fori_loop(0, 1, cross_tile, jnp.zeros((8, BLK), F32))
@@ -259,15 +381,8 @@
     wide_recv(2, b1w)
     narrow_recv(2, a1n)
 
-    @pl.when(lax.div(n, 2) != w)
-    def _():
-        wide_copy(4, lax.rem(w - lax.div(n, 2) + WN, WN), va, Dn).wait_recv()
-    for h in (0, 1):
-        @pl.when(n != 2 * w + h)
-        def _():
-            narrow_copy(4, lax.rem(n - 2 * w - h + NN, NN), vb, Dw.at[h]).wait_recv()
-
-    vec = lambda r, i: [Dw[h, i:i + 1, :] for h in (0, 1)]
+    diag_recv()
+
     dmean, dinv, dd = (stacked([Dw[h, i:i + 1, :] for h in (0, 1)]) for i in range(3))
     for i in range(WN):
         s = ((b1w[i].astype(F32) - dmean) * dinv).astype(BF16).astype(F32) * dd
@@ -357,34 +472,44 @@
         for h in (0, 1):
             ga_ref[:, i * SLAB + h * HS:i * SLAB + (h + 1) * HS] = rar[i, h * 8:h * 8 + 8, :]
     wide_recv(8, lrecv)
-    loss = jnp.sum(sum_messages(lrecv), keepdims=True) / FEATS
-    loss_ref[...] = jnp.broadcast_to(loss, loss_ref.shape)
+    loss_ref[...] = sum_messages(lrecv) / FEATS
     narrow_recv(7, rbr)
     for i in range(NN):
         for h in (0, 1):
             gb_ref[:, i * BLK + h * HB:i * BLK + (h + 1) * HB] = rbr[i, h * 8:h * 8 + 8, :]
 
-    wide_sent(0, xa.at[0])
-    narrow_sent(0, xb.at[0])
-    wide_sent(1, B3.at[0])
-    narrow_sent(1, A3.at[0])
-    wide_sent(2, xb2.at[0])
-    narrow_sent(2, xa2.at[0])
-    wide_sent(3, gas.at[0])
-    narrow_sent(3, gbs.at[0])
-
-    @pl.when(diag)
-    def _():
-        wide_sent(4, va)
-        narrow_sent(4, vb)
-    wide_sent(5, gball.at[0])
-    narrow_sent(5, gaall.at[0])
-    wide_sent(6, mbs)
-    narrow_sent(6, mas)
-    wide_sent(7, ras.at[0])
-    narrow_sent(7, rbs.at[0])
-    wide_sent(8, lsend)
-    lax.fori_loop(0, tiles, lambda i, c: (corr_out(i).wait(), c)[1], 0)
+    wide_sent(0, A3.at[n])
+    narrow_sent(0, B3.at[w])
+    wide_sent(1, B3)
+    narrow_sent(1, A3)
+    wide_sent(2, b1w)
+    narrow_sent(2, a1n)
+    wide_sent(3, gar)
+    narrow_sent(3, gbr)
+    diag_sent()
+    wide_sent(5, gball)
+    narrow_sent(5, gaall)
+    wide_sent(6, mbr)
+    narrow_sent(6, mar)
+    wide_sent(7, rar)
+    narrow_sent(7, rbr)
+    wide_sent(8, lrecv)
+
+
+def write_out(corr, loss, ga, gb, corr_out, loss_out, ga_out, gb_out, sem):
+    rows = corr.shape[0] // 8
+    copies = [
+        pltpu.make_async_copy(
+            corr.at[pl.ds(i * rows, rows)], corr_out.at[pl.ds(i * rows, rows)], sem.at[i])
+        for i in range(8)
+    ]
+    copies.append(pltpu.make_async_copy(ga, ga_out, sem.at[8]))
+    copies.append(pltpu.make_async_copy(gb, gb_out, sem.at[9]))
+    for copy in copies:
+        copy.start()
+    loss_out[0, 0] = jnp.sum(loss[...])
+    for copy in copies:
+        copy.wait()
 
 
 def solution(mesh):
@@ -398,17 +523,21 @@
         HB, HS, HN = BLK // 2, SLAB // 2, samples // 2
         V = pltpu.VMEM
         vmem = pl.BlockSpec(memory_space=pltpu.VMEM)
+        hbm = pl.BlockSpec(memory_space=pltpu.HBM)
+        anywhere = pl.BlockSpec(memory_space=pl.ANY)
+        dma = pltpu.SemaphoreType.DMA
         corr, loss, ga, gb = pl.pallas_call(
             functools.partial(kernel, WN, NN, BLK, samples),
             out_shape=(
-                jax.ShapeDtypeStruct((SLAB, BLK), BF16),
-                jax.ShapeDtypeStruct((8, 128), F32),
-                jax.ShapeDtypeStruct((rows, features), BF16),
-                jax.ShapeDtypeStruct((rows, features), BF16),
+                V((SLAB, BLK), BF16),
+                V((8, BLK // 2), F32),
+                V((rows, features), BF16),
+                V((rows, features), BF16),
             ),
-            in_specs=[vmem, vmem],
-            out_specs=(pl.BlockSpec(memory_space=pl.ANY), vmem, vmem, vmem),
+            in_specs=[hbm, hbm],
+            out_specs=(vmem, vmem, vmem, vmem),
             scratch_shapes=[
+                V((rows, features), BF16), V((rows, features), BF16), V((NN, 8, BLK), F32),
                 V((WN, 16, HS), BF16), V((NN, 16, HB), BF16),
                 V((WN, 16, HS), BF16), V((NN, 16, HB), BF16),
                 V((NN, WN, 16, HS), BF16), V((WN, NN, 16, HB), BF16),
@@ -423,15 +552,26 @@
                 V((WN, 16, HS), BF16), V((WN, 16, HS), BF16),
                 V((NN, 16, HB), BF16), V((NN, 16, HB), BF16),
                 V((8, BLK), F32), V((8, BLK // 2), F32), V((WN, 8, BLK // 2), F32),
-                V((SLAB, BLK), BF16),
-                pltpu.SemaphoreType.DMA((9, WN)), pltpu.SemaphoreType.DMA((9, WN)),
-                pltpu.SemaphoreType.DMA((9, NN)), pltpu.SemaphoreType.DMA((9, NN)),
-                pltpu.SemaphoreType.DMA((8,)),
+                dma((9,)), dma((9,)), dma((9,)), dma((9,)),
+                dma((2, 20)), dma((7,)), dma((2,)), dma((2,)),
             ],
             compiler_params=pltpu.CompilerParams(
-                collective_id=0, has_side_effects=True, vmem_limit_bytes=56 * 1024 * 1024),
-        )(view_a, view_b)
-        return corr, loss[0, 0], ga, gb
+                collective_id=0, has_side_effects=True, vmem_limit_bytes=32 * 1024 * 1024),
+        )(*(pltpu.with_memory_space_constraint(v, pltpu.HBM) for v in (view_a, view_b)))
+        corr, loss, ga, gb = pl.pallas_call(
+            write_out,
+            out_shape=(
+                jax.ShapeDtypeStruct((SLAB, BLK), BF16),
+                jax.ShapeDtypeStruct((1, 1), F32),
+                jax.ShapeDtypeStruct((rows, features), BF16),
+                jax.ShapeDtypeStruct((rows, features), BF16),
+            ),
+            in_specs=[anywhere, vmem, anywhere, anywhere],
+            out_specs=(anywhere, pl.BlockSpec(memory_space=pltpu.SMEM), anywhere, anywhere),
+            scratch_shapes=[dma((10,))],
+            compiler_params=pltpu.CompilerParams(vmem_limit_bytes=8 * 1024 * 1024),
+        )(corr, loss, ga, gb)
+        return corr, loss.reshape(()), ga, gb
 
     return jax.shard_map(
         on_device,

time: 79.4 us -> 53.4 us (0.67)
  Pallas kernels: 73.5 us -> 52.5 us
  local copies, waits for them, and re-layouts: 5.1 us -> 0 us
    pallas_call x1, Pallas kernels: 73.5 us -> 50.8 us  [on_device(): pl.pallas_call(functools.partial(kernel, WN, NN, BLK, samples), out_shape...]
    unnamed x7 -> x0, local copies, waits for them, and re-layouts: 3.91 us -> none
    pallas_call x0 -> x1, Pallas kernels: none -> 1.65 us  [on_device(): pl.pallas_call(write_out, out_shape=(jax.ShapeDtypeStruct((SLAB, BLK), BF...]
    slice x1 -> x0, local copies, waits for them, and re-layouts: 1.2 us -> none  [on_device(): return (corr, loss[0, 0], ga, gb)]
where the time goes in v2:
time: 53.4 us; the launch traced here: 53.1 us
  Pallas kernels  52.5 us (98%)
  between operations  0.64 us (1%)
    pallas_call x1, Pallas kernels, on_device(): pl.pallas_call(functools.partial(kernel, WN, NN, BLK, samples), out_shape...  50.8 us
    pallas_call x1, Pallas kernels, on_device(): pl.pallas_call(write_out, out_shape=(jax.ShapeDtypeStruct((SLAB, BLK), BF...  1.65 us

profile of v2, /device:TPU:0, one launch (start us, length us, event | category | flops | bytes accessed | tf_op | source)
XLA Modules:
  0.0 53.1 jit_solution(14686534871699678857)
XLA Ops:
  0.6 50.8 %shard_map.57 = (bf16[1024,512]{1,0:T(8,128)(2,1)S(1)}, f32[8,256]{1,0:T(8,128)S(1)}, bf16[8,8192]{1,0:T(8,128)(2,1)S(1)}, bf16[8,8192]{1,0:T(8,128)(2,1)S(1)}) custom-call(bf16[8,8192]{1,0:T(8,128)(2,1)} %a_hbm.1, bf16[8,8192]{1,0:T(8,128)(2,1)} %b_hbm.1), custom_call_target="tpu_custom_call" | custom-call | tf_op jit(solution)/shard_map/pallas_call | solution.py:529
  51.5 1.6 %shard_map.58 = (bf16[1024,512]{1,0:T(8,128)(2,1)}, f32[1,1]{1,0:T(1,128)}, bf16[8,8192]{1,0:T(8,128)(2,1)}, bf16[8,8192]{1,0:T(8,128)(2,1)}) custom-call(bf16[1024,512]{1,0:T(8,128)(2,1)S(1)} %get-tuple-element.12.corr, f32[8,256]{1,0:T(8,128)S(1)} %get-tuple-element.13.loss, bf16[8,8192]{1,0:T(8,128)(2,1)S(1)} %get-tuple-element.14.ga, ...), custom_call_target="tpu_custom_call" | custom-call | tf_op jit(solution)/shard_map/pallas_call | solution.py:561

commit v3 on v2

--- a/solution.py
+++ b/solution.py
@@ -25,7 +25,7 @@
     gas, gar, gaall, gbs, gbr, gball,
     va, vb, Dn, Dw,
     dA, dB,
-    mas, mar, mbs, mbr,
+    mas, mar, mbs, mbr, ea, eb,
     ras, rar, rbs, rbr,
     lbuf, lsend, lrecv,
     s_w, r_w, s_n, r_n, r_a, r_b, r_d, in_sem,
@@ -38,23 +38,35 @@
     n = lax.axis_index("narrow")
     diag = lax.div(n, 2) == w
 
+    z, y = lax.div(n, 4), lax.rem(n, 4)
+    x, core = lax.div(w, 2), lax.rem(w, 2)
+
+    def offset(j):
+        return lax.rem(2 + 3 * j + 3 * lax.div(j * (j - 1), 2), 4)
+
+    def wide_peer(i):
+        return lax.rem(x + offset(lax.div(i, 2)), 4) * 2 + lax.rem(core + 1 - lax.rem(i, 2), 2)
+
+    def narrow_peer(i):
+        return lax.rem(z + offset(lax.div(i, 4)), 4) * 4 + lax.rem(y + offset(lax.rem(i, 4)), 4)
+
     def wide_copy(which, k, src, dst):
         return pltpu.make_async_remote_copy(
             src_ref=src, dst_ref=dst, send_sem=s_w.at[which], recv_sem=r_w.at[which],
-            device_id=(lax.rem(w + k, WN), n), device_id_type=MESH,
+            device_id=(wide_peer(k), n), device_id_type=MESH,
         )
 
     def narrow_copy(which, k, src, dst):
         return pltpu.make_async_remote_copy(
             src_ref=src, dst_ref=dst, send_sem=s_n.at[which], recv_sem=r_n.at[which],
-            device_id=(w, lax.rem(n + k, NN)), device_id_type=MESH,
+            device_id=(w, narrow_peer(k)), device_id_type=MESH,
         )
 
     def each(count, body):
         def step(k, c):
             body(k)
             return c
-        lax.fori_loop(1, count, step, 0)
+        lax.fori_loop(0, count - 1, step, 0)
 
 
     def wide_recv(which, dst):
@@ -74,10 +86,10 @@
         narrow_copy(which, 1, ref, ref).wait_send()
 
     def wide_a2a(which, src, dst):
-        each(WN, lambda k: wide_copy(which, k, src.at[lax.rem(w + k, WN)], dst.at[w]).start())
+        each(WN, lambda k: wide_copy(which, k, src.at[wide_peer(k)], dst.at[w]).start())
 
     def narrow_a2a(which, src, dst):
-        each(NN, lambda k: narrow_copy(which, k, src.at[lax.rem(n + k, NN)], dst.at[n]).start())
+        each(NN, lambda k: narrow_copy(which, k, src.at[narrow_peer(k)], dst.at[n]).start())
 
     def wide_bcast(which, src, dst):
         each(WN, lambda k: wide_copy(which, k, src, dst.at[w]).start())
@@ -93,9 +105,9 @@
         load.start()
     barrier = pltpu.get_barrier_semaphore()
     each(WN, lambda k: pl.semaphore_signal(
-        barrier, inc=1, device_id=(lax.rem(w + k, WN), n), device_id_type=MESH))
+        barrier, inc=1, device_id=(wide_peer(k), n), device_id_type=MESH))
     each(NN, lambda k: pl.semaphore_signal(
-        barrier, inc=1, device_id=(w, lax.rem(n + k, NN)), device_id_type=MESH))
+        barrier, inc=1, device_id=(w, narrow_peer(k)), device_id_type=MESH))
 
     for load in loads:
         load.wait()
@@ -120,8 +132,6 @@
         xa2[i] = stack(a_ref, i * BLK, HB)
     b1w[w] = xb2[w]
     a1n[n] = xa2[n]
-    z, y = lax.div(n, 4), lax.rem(n, 4)
-    x, core = lax.div(w, 2), lax.rem(w, 2)
     PART = WN // 2
     FULL, FIRST, SECOND = (0, PART), (0, PART // 2), (PART // 2, PART // 2)
 
@@ -275,7 +285,6 @@
         for part in (0, 1):
             far(part, line, LINES[line], 2)
             sums_a = sums_of_piece(part, slot(part, LINES[line], 2), sums_a)
-    narrow_a2a(2, xa2, a1n)
     mean_a, inv_a = moments_of(sums_a)
     mean2a, inv2a = stacked(mean_a), stacked(inv_a)
 
@@ -300,14 +309,21 @@
     wide_a2a(3, gas, gar)
     gar[w] = gas[w]
 
+    narrow_a2a(2, xa2, a1n)
+    ones = jnp.ones((8, SAMPLES), BF16)
+    mstd_a = jnp.dot(ones, S_a[...], preferred_element_type=F32) / SAMPLES
+    mstd_b = jnp.dot(ones, S_b[...], preferred_element_type=F32) / SAMPLES
+
     half = lax.rem(n, 2)
     lbuf[...] = jnp.zeros_like(lbuf)
+    ea[...] = jnp.zeros_like(ea)
+    eb[...] = jnp.zeros_like(eb)
 
     def narrow_vec(k, h=None):
         h = half if h is None else h
         return pltpu.make_async_remote_copy(
             src_ref=vb, dst_ref=Dw.at[h], send_sem=s_n.at[4], recv_sem=r_d.at[h],
-            device_id=(w, lax.rem(n + k, NN)), device_id_type=MESH,
+            device_id=(w, narrow_peer(k)), device_id_type=MESH,
         )
 
     @pl.when(diag)
@@ -324,6 +340,10 @@
         first = (half == 0).astype(F32)
         ma = mean_a[0] * first + mean_a[1] * (1.0 - first)
         ia = inv_a[0] * first + inv_a[1] * (1.0 - first)
+        msa = mstd_a[0:1, :BLK] * first + mstd_a[0:1, BLK:] * (1.0 - first)
+        pad = jnp.zeros((6, BLK), F32)
+        ea[half] = jnp.concatenate([d * mstd_b[0:1], d * c, pad], axis=0)
+        eb[...] = jnp.concatenate([d * msa, d * c, pad], axis=0)
         pad = jnp.zeros((5, BLK), F32)
         va[...] = jnp.concatenate([ma, ia, d, pad], axis=0)
         vb[...] = jnp.concatenate([mb, ib, d, pad], axis=0)
@@ -350,33 +370,53 @@
             ref = dummy.at[pl.ds(0, NN - 1)]
             narrow_copy(4, 1, ref, ref).wait_send()
 
-    narrow_recv(3, gbr)
+    TM = SLAB // 2
+    acc = jnp.zeros((8, BLK), F32)
+    fb = jnp.zeros((8, BLK), F32)
+    ones = jnp.ones((8, BLK), BF16)
+    msb = mstd_b.astype(BF16)
+    fa, sa = [], []
+    for t in range(2):
+        at = slice(t * TM, (t + 1) * TM)
+        c = lax.dot_general(
+            S_a[:, at], S_b[...], (((0,), (0,)), ((), ())), preferred_element_type=F32
+        ) * (1.0 / SAMPLES)
+        rounded = c.astype(BF16)
+        corr_ref[at, :] = rounded
+        squares = c * c
+        acc = acc + jnp.sum(squares.reshape(TM // 8, 8, BLK), axis=0)
+        fa.append(dot_last(msb, rounded)[0:1])
+        sa.append(dot_last(ones, squares.astype(BF16))[0:1])
+        fb = fb + jnp.dot(mstd_a[:, at].astype(BF16), rounded, preferred_element_type=F32)
+    twice = 2.0 * off_weight
+    m1 = jnp.concatenate([twice * fa[h] + ea[h, 0:1] for h in (0, 1)], axis=1)
+    m2 = jnp.concatenate([twice * sa[h] + ea[h, 1:2] for h in (0, 1)], axis=1)
+    Q = SLAB // 4
+    lost = lbuf[...] + off_weight * acc
+    mas[...] = jnp.concatenate(
+        [jnp.concatenate([m[:, q * Q:(q + 1) * Q] for m in (m1, m2) for q in range(4)], axis=0)]
+        + [sum(lost[:, q * 128:(q + 1) * 128] for q in range(BLK // 128))], axis=1)
+    narrow_bcast(6, mas, mar)
+    mar[n] = mas[...]
+    m1 = twice * fb[0:1] + eb[0:1]
+    m2 = twice * jnp.sum(acc, axis=0, keepdims=True) + eb[1:2]
+    QB = BLK // 4
+    mbs[...] = jnp.concatenate(
+        [m[:, q * QB:(q + 1) * QB] for m in (m1, m2) for q in range(4)], axis=0)
+    wide_bcast(6, mbs, mbr)
+    mbr[w] = mbs[...]
 
     def total_of(ref):
         t = ref[0].astype(F32)
         for i in range(1, ref.shape[0]):
             t = t + ref[i].astype(F32)
         return t
-    gball[w] = total_of(gbr).astype(BF16)
-    wide_bcast(5, gball.at[w], gball)
-
-    TM = 256 if SLAB % 256 == 0 else SLAB
-
-    def cross_tile(i, acc):
-        at = pl.ds(pl.multiple_of(i * TM, TM), TM)
-        c = lax.dot_general(
-            S_a[:, at], S_b[...], (((0,), (0,)), ((), ())), preferred_element_type=F32
-        ) * (1.0 / SAMPLES)
-        corr_ref[at, :] = c.astype(BF16)
-        return acc + jnp.sum((c * c).reshape(TM // 8, 8, BLK), axis=0)
-    tiles = SLAB // TM
-    acc = lax.fori_loop(0, 1, cross_tile, jnp.zeros((8, BLK), F32))
-
     wide_recv(3, gar)
     gaall[n] = total_of(gar).astype(BF16)
     narrow_bcast(5, gaall.at[n], gaall)
-    acc = lax.fori_loop(1, tiles, cross_tile, acc)
-    lbuf[...] = lbuf[...] + off_weight * acc
+    narrow_recv(3, gbr)
+    gball[w] = total_of(gbr).astype(BF16)
+    wide_bcast(5, gball.at[w], gball)
 
     wide_recv(2, b1w)
     narrow_recv(2, a1n)
@@ -410,57 +450,39 @@
 
     wide_recv(5, gball)
     g0, g1 = unstack(gball)
-    Q = SLAB // 4
     d = factor * (
         jnp.dot(g0, S_a[:HN, :], preferred_element_type=F32)
         + jnp.dot(g1, S_a[HN:, :], preferred_element_type=F32)
     ) + dA[...]
-    dA[...] = d
-    m1 = jnp.sum(d, axis=0, keepdims=True)
-    m2 = jnp.sum(d * SR_a[...].astype(F32), axis=0, keepdims=True)
-    mas[0:8, :] = jnp.concatenate(
-        [m[:, q * Q:(q + 1) * Q] for m in (m1, m2) for q in range(4)], axis=0)
-    mas[8:16, :] = lbuf[:, :BLK // 2] + lbuf[:, BLK // 2:]
-    narrow_bcast(6, mas, mar)
-    mar[n] = mas[...]
-
-    narrow_recv(5, gaall)
-    g0, g1 = unstack(gaall)
-    own = pl.ds(pl.multiple_of(w * NN * 8, 16), NN * 8)
-    d = factor * (
-        jnp.dot(g0, S_b[:HN, :], preferred_element_type=F32)
-        + jnp.dot(g1, S_b[HN:, :], preferred_element_type=F32)
-    ) + dB[...]
-    dB[...] = d
-    m1 = jnp.sum(d, axis=0, keepdims=True)
-    m2 = jnp.sum(d * S_b[own, :].astype(F32), axis=0, keepdims=True)
-    QB = BLK // 4
-    mbs[...] = jnp.concatenate(
-        [m[:, q * QB:(q + 1) * QB] for m in (m1, m2) for q in range(4)], axis=0)
-    wide_bcast(6, mbs, mbr)
-    mbr[w] = mbs[...]
-
     narrow_recv(6, mar)
-    total = sum_messages(mar) / SAMPLES
-    m1 = jnp.concatenate([total[q:q + 1] for q in range(4)], axis=1)
-    m2 = jnp.concatenate([total[q + 4:q + 5] for q in range(4)], axis=1)
+    total = sum_messages(mar)
+    m1 = jnp.concatenate([total[q:q + 1, :Q] for q in range(4)], axis=1)
+    m2 = jnp.concatenate([total[q + 4:q + 5, :Q] for q in range(4)], axis=1)
     inv = jnp.concatenate(inv_a, axis=1)
-    grad = inv * (dA[...] - m1 - SR_a[...].astype(F32) * m2)
+    grad = inv * (d - m1 - SR_a[...].astype(F32) * m2)
     for i in range(WN):
         ras[i] = jnp.concatenate(
             [grad[i * 8:i * 8 + 8, h * HS:(h + 1) * HS] for h in (0, 1)], axis=0).astype(BF16)
     wide_a2a(7, ras, rar)
     rar[w] = ras[w]
-    lsend[...] = total[8:16] * SAMPLES
+    lsend[...] = total[:, Q:]
     wide_bcast(8, lsend, lrecv)
     lrecv[w] = lsend[...]
 
     wide_recv(6, mbr)
-    total = sum_messages(mbr) / SAMPLES
+    total = sum_messages(mbr)
     m1 = jnp.concatenate([total[q:q + 1] for q in range(4)], axis=1)
     m2 = jnp.concatenate([total[q + 4:q + 5] for q in range(4)], axis=1)
     inv = jnp.concatenate(inv_b, axis=1)
-    grad = inv * (dB[...] - m1 - S_b[own, :].astype(F32) * m2)
+    own = pl.ds(pl.multiple_of(w * NN * 8, 16), NN * 8)
+    rest = dB[...] - m1 - S_b[own, :].astype(F32) * m2
+    narrow_recv(5, gaall)
+    g0, g1 = unstack(gaall)
+    d = factor * (
+        jnp.dot(g0, S_b[:HN, :], preferred_element_type=F32)
+        + jnp.dot(g1, S_b[HN:, :], preferred_element_type=F32)
+    )
+    grad = inv * (d + rest)
     for i in range(NN):
         rbs[i] = jnp.concatenate(
             [grad[i * 8:i * 8 + 8, h * HB:(h + 1) * HB] for h in (0, 1)], axis=0).astype(BF16)
@@ -530,7 +552,7 @@
             functools.partial(kernel, WN, NN, BLK, samples),
             out_shape=(
                 V((SLAB, BLK), BF16),
-                V((8, BLK // 2), F32),
+                V((8, 128), F32),
                 V((rows, features), BF16),
                 V((rows, features), BF16),
             ),
@@ -547,11 +569,12 @@
                 V((NN, 16, HN), BF16), V((NN, 16, HN), BF16), V((WN, 16, HN), BF16),
                 V((8, BLK), F32), V((8, BLK), F32), V((8, BLK), F32), V((2, 8, BLK), F32),
                 V((WN * 8, SLAB), F32), V((NN * 8, BLK), F32),
-                V((16, SLAB // 4), F32), V((NN, 16, SLAB // 4), F32),
+                V((8, SLAB // 4 + 128), F32), V((NN, 8, SLAB // 4 + 128), F32),
                 V((8, BLK // 4), F32), V((WN, 8, BLK // 4), F32),
+                V((2, 8, BLK), F32), V((8, BLK), F32),
                 V((WN, 16, HS), BF16), V((WN, 16, HS), BF16),
                 V((NN, 16, HB), BF16), V((NN, 16, HB), BF16),
-                V((8, BLK), F32), V((8, BLK // 2), F32), V((WN, 8, BLK // 2), F32),
+                V((8, BLK), F32), V((8, 128), F32), V((WN, 8, 128), F32),
                 dma((9,)), dma((9,)), dma((9,)), dma((9,)),
                 dma((2, 20)), dma((7,)), dma((2,)), dma((2,)),
             ],

time: 53.4 us -> 48.8 us (0.914)
  Pallas kernels: 52.5 us -> 48.1 us
    pallas_call x1, Pallas kernels: 50.8 us -> 46.4 us  [on_device(): pl.pallas_call(functools.partial(kernel, WN, NN, BLK, samples), out_shape...]
where the time goes in v3:
time: 48.8 us; the launch traced here: 48.7 us
  Pallas kernels  48.1 us (99%)
  between operations  0.64 us (1%)
    pallas_call x1, Pallas kernels, on_device(): pl.pallas_call(functools.partial(kernel, WN, NN, BLK, samples), out_shape...  46.4 us
    pallas_call x1, Pallas kernels, on_device(): pl.pallas_call(write_out, out_shape=(jax.ShapeDtypeStruct((SLAB, BLK), BF...  1.65 us

profile of v3, /device:TPU:0, one launch (start us, length us, event | category | flops | bytes accessed | tf_op | source)
XLA Modules:
  0.0 48.7 jit_solution(4917672598294348855)
XLA Ops:
  0.6 46.4 %shard_map.57 = (bf16[1024,512]{1,0:T(8,128)(2,1)S(1)}, f32[8,128]{1,0:T(8,128)S(1)}, bf16[8,8192]{1,0:T(8,128)(2,1)S(1)}, bf16[8,8192]{1,0:T(8,128)(2,1)S(1)}) custom-call(bf16[8,8192]{1,0:T(8,128)(2,1)} %a_hbm.1, bf16[8,8192]{1,0:T(8,128)(2,1)} %b_hbm.1), custom_call_target="tpu_custom_call" | custom-call | tf_op jit(solution)/shard_map/pallas_call | solution.py:551
  47.1 1.6 %shard_map.58 = (bf16[1024,512]{1,0:T(8,128)(2,1)}, f32[1,1]{1,0:T(1,128)}, bf16[8,8192]{1,0:T(8,128)(2,1)}, bf16[8,8192]{1,0:T(8,128)(2,1)}) custom-call(bf16[1024,512]{1,0:T(8,128)(2,1)S(1)} %get-tuple-element.12.corr, f32[8,128]{1,0:T(8,128)S(1)} %get-tuple-element.13.loss, bf16[8,8192]{1,0:T(8,128)(2,1)S(1)} %get-tuple-element.14.ga, ...), custom_call_target="tpu_custom_call" | custom-call | tf_op jit(solution)/shard_map/pallas_call | solution.py:584

commit v4 on v3

--- a/solution.py
+++ b/solution.py
@@ -122,8 +122,8 @@
         xb[i] = stack(b_ref, i * BLK, HB)
     pl.semaphore_wait(barrier, WN + NN - 2)
 
+    narrow_a2a(0, xb, B3.at[w])
     wide_a2a(0, xa, A3.at[n])
-    narrow_a2a(0, xb, B3.at[w])
     A3[n, w] = xa[w]
     B3[w, n] = xb[n]
     for i in range(WN):
@@ -153,7 +153,7 @@
 
     def along(part, line, p, stage):
         step = (lambda d: (d, 0)) if stage == 1 else (lambda d: (0, d))
-        for d, index in ((1, 0), (-1, 1)):
+        for d, index in ((2, 3), (1, 0), (-1, 1)) if line == 3 else ((1, 0), (-1, 1)):
             move(part, line * 4 + index, slot(part, p, 0), FULL, *step(d)).start()
 
     def relay(part, line, p, stage):
@@ -161,11 +161,12 @@
             got = slot(part, -d, 0) if stage == 1 else slot(part, p, -d)
             step = (d, 0) if stage == 1 else (0, d)
             move(part, line * 4 + index - 2, got, FULL, 0, 0).wait_recv()
-            move(part, line * 4 + index, got, cut, *step).start()
+            if line != 3:
+                move(part, line * 4 + index, got, cut, *step).start()
 
     def far(part, line, p, stage):
         got = slot(part, 2, 0) if stage == 1 else slot(part, p, 2)
-        for index, cut in ((2, FIRST), (3, SECOND)):
+        for index, cut in ((3, FULL),) if line == 3 else ((2, FIRST), (3, SECOND)):
             move(part, line * 4 + index, got, cut, 0, 0).wait_recv()
 
     def move_b(index, at, dx, other):
@@ -188,8 +189,6 @@
     for i, dx in enumerate((1, -1, 2)):
         move_b(i, w, dx, False).start()
     move_b(3, w, 0, True).start()
-    wide_a2a(2, xb2, b1w)
-
     def add_sums(ref, sums):
         def step(i, c):
             v = ref[i].astype(F32)
@@ -240,44 +239,45 @@
         for line in (1, 2):
             relay(part, line, LINES[line], 2)
     sums_b = take_b(2, 2, sums_b)
+    for i, dx in ((3, 0), (4, 1), (5, -1), (6, 2)):
+        move_b(i, slot_b(-dx, True), 0, True).wait_recv()
+        sums_b = add_sums(B3.at[slot_b(-dx, True)], sums_b)
+    mean_b, inv_b = moments_of(sums_b)
+    mean2, inv2 = stacked(mean_b), stacked(inv_b)
+
+    def norm_b(i, c):
+        src, pair = lax.div(i, NN // 2), lax.rem(i, NN // 2)
+        even = (B3[src, 2 * pair].astype(F32) - mean2) * inv2
+        odd = (B3[src, 2 * pair + 1].astype(F32) - mean2) * inv2
+        at = pl.ds(pl.multiple_of(i * 16, 16), 16)
+        for h in (0, 1):
+            S_b[at, h * HB:(h + 1) * HB] = jnp.concatenate(
+                [even[h * 8:h * 8 + 8], odd[h * 8:h * 8 + 8]], axis=0).astype(BF16)
+        return c
+    lax.fori_loop(0, SAMPLES // 16, norm_b, 0, unroll=2)
+
+    dot_last = functools.partial(
+        lax.dot_general, dimension_numbers=(((1,), (1,)), ((), ())), preferred_element_type=F32)
+
+    def stack_gram(dst, g):
+        count = g.shape[0] // 8
+        g3 = g.reshape(count, 8, SAMPLES)
+        dst[...] = jnp.concatenate([g3[:, :, :HN], g3[:, :, HN:]], axis=1).astype(BF16)
+
+    own_rows = S_b[pl.ds(pl.multiple_of(w * NN * 8, 16), NN * 8), :]
+    stack_gram(gbs, dot_last(own_rows, S_b[...]))
+    narrow_a2a(3, gbs, gbr)
+    gbr[n] = gbs[n]
+    for part in (0, 1):
+        relay(part, 3, 2, 2)
+    wide_a2a(2, xb2, b1w)
+
     for part in (0, 1):
         for q in (-1, 1):
             sums_a = sums_of_piece(part, slot(part, 0, q), sums_a)
             for p in (-1, 1):
                 sums_a = sums_of_piece(part, slot(part, p, q), sums_a)
         sums_a = sums_of_piece(part, slot(part, 2, 0), sums_a)
-    for i, dx in ((3, 0), (4, 1), (5, -1), (6, 2)):
-        move_b(i, slot_b(-dx, True), 0, True).wait_recv()
-        sums_b = add_sums(B3.at[slot_b(-dx, True)], sums_b)
-    for part in (0, 1):
-        relay(part, 3, 2, 2)
-    mean_b, inv_b = moments_of(sums_b)
-    mean2, inv2 = stacked(mean_b), stacked(inv_b)
-
-    def norm_b(i, c):
-        src, pair = lax.div(i, NN // 2), lax.rem(i, NN // 2)
-        even = (B3[src, 2 * pair].astype(F32) - mean2) * inv2
-        odd = (B3[src, 2 * pair + 1].astype(F32) - mean2) * inv2
-        at = pl.ds(pl.multiple_of(i * 16, 16), 16)
-        for h in (0, 1):
-            S_b[at, h * HB:(h + 1) * HB] = jnp.concatenate(
-                [even[h * 8:h * 8 + 8], odd[h * 8:h * 8 + 8]], axis=0).astype(BF16)
-        return c
-    lax.fori_loop(0, SAMPLES // 16, norm_b, 0, unroll=2)
-
-    dot_last = functools.partial(
-        lax.dot_general, dimension_numbers=(((1,), (1,)), ((), ())), preferred_element_type=F32)
-
-    def stack_gram(dst, g):
-        count = g.shape[0] // 8
-        g3 = g.reshape(count, 8, SAMPLES)
-        dst[...] = jnp.concatenate([g3[:, :, :HN], g3[:, :, HN:]], axis=1).astype(BF16)
-
-    own_rows = S_b[pl.ds(pl.multiple_of(w * NN * 8, 16), NN * 8), :]
-    stack_gram(gbs, dot_last(own_rows, S_b[...]))
-    narrow_a2a(3, gbs, gbr)
-    gbr[n] = gbs[n]
-
     for part in (0, 1):
         for q in (-1, 1):
             sums_a = sums_of_piece(part, slot(part, 2, q), sums_a)
@@ -494,7 +494,8 @@
         for h in (0, 1):
             ga_ref[:, i * SLAB + h * HS:i * SLAB + (h + 1) * HS] = rar[i, h * 8:h * 8 + 8, :]
     wide_recv(8, lrecv)
-    loss_ref[...] = sum_messages(lrecv) / FEATS
+    loss = jnp.sum(sum_messages(lrecv), keepdims=True) / FEATS
+    loss_ref[...] = jnp.broadcast_to(loss, loss_ref.shape)
     narrow_recv(7, rbr)
     for i in range(NN):
         for h in (0, 1):
@@ -527,9 +528,9 @@
     ]
     copies.append(pltpu.make_async_copy(ga, ga_out, sem.at[8]))
     copies.append(pltpu.make_async_copy(gb, gb_out, sem.at[9]))
+    copies.append(pltpu.make_async_copy(loss.at[pl.ds(0, 1)], loss_out, sem.at[10]))
     for copy in copies:
         copy.start()
-    loss_out[0, 0] = jnp.sum(loss[...])
     for copy in copies:
         copy.wait()
 
@@ -585,16 +586,16 @@
             write_out,
             out_shape=(
                 jax.ShapeDtypeStruct((SLAB, BLK), BF16),
-                jax.ShapeDtypeStruct((1, 1), F32),
+                jax.ShapeDtypeStruct((1, 128), F32),
                 jax.ShapeDtypeStruct((rows, features), BF16),
                 jax.ShapeDtypeStruct((rows, features), BF16),
             ),
-            in_specs=[anywhere, vmem, anywhere, anywhere],
-            out_specs=(anywhere, pl.BlockSpec(memory_space=pltpu.SMEM), anywhere, anywhere),
-            scratch_shapes=[dma((10,))],
+            in_specs=[anywhere] * 4,
+            out_specs=(anywhere,) * 4,
+            scratch_shapes=[dma((11,))],
             compiler_params=pltpu.CompilerParams(vmem_limit_bytes=8 * 1024 * 1024),
         )(corr, loss, ga, gb)
-        return corr, loss.reshape(()), ga, gb
+        return corr, loss[0, 0], ga, gb
 
     return jax.shard_map(
         on_device,

time: 48.8 us -> 48.2 us (0.988)
  Pallas kernels: 48.1 us -> 47.4 us
    pallas_call x1, Pallas kernels: 1.65 us -> 1.14 us  [on_device(): pl.pallas_call(write_out, out_shape=(jax.ShapeDtypeStruct((SLAB, BLK), BF...]
where the time goes in v4:
time: 48.2 us; the launch traced here: 48 us
  Pallas kernels  47.4 us (98%)
  between operations  0.64 us (1%)
    pallas_call x1, Pallas kernels, on_device(): pl.pallas_call(functools.partial(kernel, WN, NN, BLK, samples), out_shape...  46.2 us
    pallas_call x1, Pallas kernels, on_device(): pl.pallas_call(write_out, out_shape=(jax.ShapeDtypeStruct((SLAB, BLK), BF...  1.14 us

profile of v4, /device:TPU:0, one launch (start us, length us, event | category | flops | bytes accessed | tf_op | source)
XLA Modules:
  0.0 48.0 jit_solution(11346077888520118009)
XLA Ops:
  0.6 46.2 %shard_map.57 = (bf16[1024,512]{1,0:T(8,128)(2,1)S(1)}, f32[8,128]{1,0:T(8,128)S(1)}, bf16[8,8192]{1,0:T(8,128)(2,1)S(1)}, bf16[8,8192]{1,0:T(8,128)(2,1)S(1)}) custom-call(bf16[8,8192]{1,0:T(8,128)(2,1)} %a_hbm.1, bf16[8,8192]{1,0:T(8,128)(2,1)} %b_hbm.1), custom_call_target="tpu_custom_call" | custom-call | tf_op jit(solution)/shard_map/pallas_call | solution.py:552
  46.9 1.1 %shard_map.58 = (bf16[1024,512]{1,0:T(8,128)(2,1)}, f32[1,128]{1,0:T(1,128)}, bf16[8,8192]{1,0:T(8,128)(2,1)}, bf16[8,8192]{1,0:T(8,128)(2,1)}) custom-call(bf16[1024,512]{1,0:T(8,128)(2,1)S(1)} %get-tuple-element.12.corr, f32[8,128]{1,0:T(8,128)S(1)} %get-tuple-element.13.loss, bf16[8,8192]{1,0:T(8,128)(2,1)S(1)} %get-tuple-element.14.ga, ...), custom_call_target="tpu_custom_call" | custom-call | tf_op jit(solution)/shard_map/pallas_call | solution.py:585

commit v5 on v4

--- a/solution.py
+++ b/solution.py
@@ -271,6 +271,7 @@
     for part in (0, 1):
         relay(part, 3, 2, 2)
     wide_a2a(2, xb2, b1w)
+    narrow_a2a(2, xa2, a1n)
 
     for part in (0, 1):
         for q in (-1, 1):
@@ -309,7 +310,6 @@
     wide_a2a(3, gas, gar)
     gar[w] = gas[w]
 
-    narrow_a2a(2, xa2, a1n)
     ones = jnp.ones((8, SAMPLES), BF16)
     mstd_a = jnp.dot(ones, S_a[...], preferred_element_type=F32) / SAMPLES
     mstd_b = jnp.dot(ones, S_b[...], preferred_element_type=F32) / SAMPLES
@@ -411,12 +411,12 @@
         for i in range(1, ref.shape[0]):
             t = t + ref[i].astype(F32)
         return t
+    narrow_recv(3, gbr)
+    gball[w] = total_of(gbr).astype(BF16)
+    wide_bcast(5, gball.at[w], gball)
     wide_recv(3, gar)
     gaall[n] = total_of(gar).astype(BF16)
     narrow_bcast(5, gaall.at[n], gaall)
-    narrow_recv(3, gbr)
-    gball[w] = total_of(gbr).astype(BF16)
-    wide_bcast(5, gball.at[w], gball)
 
     wide_recv(2, b1w)
     narrow_recv(2, a1n)

time: 48.2 us -> 47.9 us (level)
  no operation moved by 1% of the time
where the time goes in v5:
time: 47.9 us; the launch traced here: 47.7 us
  Pallas kernels  47.1 us (98%)
  between operations  0.64 us (1%)
    pallas_call x1, Pallas kernels, on_device(): pl.pallas_call(functools.partial(kernel, WN, NN, BLK, samples), out_shape...  46 us
    pallas_call x1, Pallas kernels, on_device(): pl.pallas_call(write_out, out_shape=(jax.ShapeDtypeStruct((SLAB, BLK), BF...  1.14 us

profile of v5, /device:TPU:0, one launch (start us, length us, event | category | flops | bytes accessed | tf_op | source)
XLA Modules:
  0.0 47.7 jit_solution(5864038990100925426)
XLA Ops:
  0.6 46.0 %shard_map.57 = (bf16[1024,512]{1,0:T(8,128)(2,1)S(1)}, f32[8,128]{1,0:T(8,128)S(1)}, bf16[8,8192]{1,0:T(8,128)(2,1)S(1)}, bf16[8,8192]{1,0:T(8,128)(2,1)S(1)}) custom-call(bf16[8,8192]{1,0:T(8,128)(2,1)} %a_hbm.1, bf16[8,8192]{1,0:T(8,128)(2,1)} %b_hbm.1), custom_call_target="tpu_custom_call" | custom-call | tf_op jit(solution)/shard_map/pallas_call | solution.py:552
  46.6 1.1 %shard_map.58 = (bf16[1024,512]{1,0:T(8,128)(2,1)}, f32[1,128]{1,0:T(1,128)}, bf16[8,8192]{1,0:T(8,128)(2,1)}, bf16[8,8192]{1,0:T(8,128)(2,1)}) custom-call(bf16[1024,512]{1,0:T(8,128)(2,1)S(1)} %get-tuple-element.12.corr, f32[8,128]{1,0:T(8,128)S(1)} %get-tuple-element.13.loss, bf16[8,8192]{1,0:T(8,128)(2,1)S(1)} %get-tuple-element.14.ga, ...), custom_call_target="tpu_custom_call" | custom-call | tf_op jit(solution)/shard_map/pallas_call | solution.py:585

commit v6 on v5

--- a/solution.py
+++ b/solution.py
@@ -186,7 +186,7 @@
     for part in (0, 1):
         along(part, 0, 0, 2)
     narrow_recv(0, B3.at[w])
-    for i, dx in enumerate((1, -1, 2)):
+    for i, dx in ((2, 2), (0, 1), (1, -1)):
         move_b(i, w, dx, False).start()
     move_b(3, w, 0, True).start()
     def add_sums(ref, sums):

time: 47.9 us -> 47.8 us (level)
  no operation moved by 1% of the time
where the time goes in v6:
time: 47.8 us; the launch traced here: 47.6 us
  Pallas kernels  47 us (98%)
  between operations  0.64 us (1%)
    pallas_call x1, Pallas kernels, on_device(): pl.pallas_call(functools.partial(kernel, WN, NN, BLK, samples), out_shape...  45.9 us
    pallas_call x1, Pallas kernels, on_device(): pl.pallas_call(write_out, out_shape=(jax.ShapeDtypeStruct((SLAB, BLK), BF...  1.14 us

profile of v6, /device:TPU:0, one launch (start us, length us, event | category | flops | bytes accessed | tf_op | source)
XLA Modules:
  0.0 47.6 jit_solution(18283731624148470407)
XLA Ops:
  0.6 45.9 %shard_map.57 = (bf16[1024,512]{1,0:T(8,128)(2,1)S(1)}, f32[8,128]{1,0:T(8,128)S(1)}, bf16[8,8192]{1,0:T(8,128)(2,1)S(1)}, bf16[8,8192]{1,0:T(8,128)(2,1)S(1)}) custom-call(bf16[8,8192]{1,0:T(8,128)(2,1)} %a_hbm.1, bf16[8,8192]{1,0:T(8,128)(2,1)} %b_hbm.1), custom_call_target="tpu_custom_call" | custom-call | tf_op jit(solution)/shard_map/pallas_call | solution.py:552
  46.5 1.1 %shard_map.58 = (bf16[1024,512]{1,0:T(8,128)(2,1)}, f32[1,128]{1,0:T(1,128)}, bf16[8,8192]{1,0:T(8,128)(2,1)}, bf16[8,8192]{1,0:T(8,128)(2,1)}) custom-call(bf16[1024,512]{1,0:T(8,128)(2,1)S(1)} %get-tuple-element.12.corr, f32[8,128]{1,0:T(8,128)S(1)} %get-tuple-element.13.loss, bf16[8,8192]{1,0:T(8,128)(2,1)S(1)} %get-tuple-element.14.ga, ...), custom_call_target="tpu_custom_call" | custom-call | tf_op jit(solution)/shard_map/pallas_call | solution.py:585
